TPU v7x, 32 devices: a whole 2x2x4 slice. The times are simulated.
32 devices in a mesh: ctx: 4 (over x, core), fsdp: 8 (over z, y).
Axes of the slice: x: 2, y: 2, z: 4, core: 2. Of those that a mesh axis runs over, the one named last changes fastest.
Arguments:
- query: bfloat16 [2, 8192, 4096], P(None, ('ctx', 'fsdp')), may hold values from -64 to 64
- key: bfloat16 [2, 8192, 2048], P(None, ('ctx', 'fsdp')), may hold values from -32 to 32
- value: bfloat16 [2, 8192, 2048], P(None, ('ctx', 'fsdp')), may hold values from -6 to 6
- grad_out: bfloat16 [2, 8192, 4096], P(None, ('ctx', 'fsdp')), may hold values from -6 to 6
- tile_start: int32 [2, 64], replicated, may hold values from 0 to 63, as said below
Outputs:
- grad_query: bfloat16 [2, 8192, 4096], P(None, ('ctx', 'fsdp'))
- grad_key: bfloat16 [2, 8192, 2048], P(None, ('ctx', 'fsdp'))
- grad_value: bfloat16 [2, 8192, 2048], P(None, ('ctx', 'fsdp'))
Inputs may be any that keep to these rules, and one draw needn't show every extreme that they name: tile_start[b, t] is the first tile of the document holding tile t: it equals t or tile_start[b, t - 1], and tile_start[b, 0] = 0; the last tile of every sequence begins a document; no document begins at a tile whose first token is a nonzero multiple of 2048.
All inputs are finite; a program needn't handle non-finite values.
Results may differ from a plain program's by a relative error of at most 0.012.
Values may be sent and summed in bfloat16 or wider, within the bound.
No kernel may reach another device: no remote copies, remote signals or barrier semaphores. Data moves between devices by JAX's collectives and lax.ppermute only.
A program may use at most 192 MiB of HBM per device.

v0:
```python
import jax
import jax.numpy as jnp
from jax import lax
from jax.sharding import PartitionSpec as P

HEADS = 32
KV_HEADS = 16
HEAD_DIM = 128
WINDOW = 1024
TILE = 128
QBLOCK = 512


score_scale = 168.0 ** (-0.5)


def partner_2(value, axis, apart):
    mask = 2**apart
    pairs = [(source, source ^ mask) for source in range(lax.axis_size(axis))]
    return lax.ppermute(value, axis, pairs)


def passed_along(shard, axis, by):
    count = lax.axis_size(axis)
    pairs = [(i, i + by) for i in range(count) if 0 <= i + by < count]
    return lax.ppermute(shard, axis, pairs)


def block_grads(q_blk, g_blk, k_span, v_span, visible):
    scores = (
        jnp.einsum("qhd,khd->hqk", q_blk, k_span, preferred_element_type=jnp.float32) * score_scale
    )
    top = jnp.max(jnp.where(visible, scores, -jnp.inf), axis=-1, keepdims=True)
    weights = jnp.exp(jnp.where(visible, scores - top, -jnp.inf))
    probs = weights / jnp.sum(weights, axis=-1, keepdims=True)
    probs_low = probs.astype(jnp.bfloat16)
    grad_probs = jnp.einsum("qhd,khd->hqk", g_blk, v_span, preferred_element_type=jnp.float32)
    delta = jnp.sum(probs * grad_probs, axis=-1, keepdims=True)
    grad_scores = (probs * (grad_probs - delta)).astype(jnp.bfloat16)
    grad_q = (
        jnp.einsum("hqk,khd->qhd", grad_scores, k_span, preferred_element_type=jnp.float32)
        * score_scale
    ).astype(jnp.bfloat16)
    grad_k = (
        jnp.einsum("hqk,qhd->khd", grad_scores, q_blk, preferred_element_type=jnp.float32)
        * score_scale
    )
    grad_v = jnp.einsum("hqk,qhd->khd", probs_low, g_blk, preferred_element_type=jnp.float32)
    return (grad_q, grad_k, grad_v)


def whole_span(operands):
    return block_grads(*operands)


def body(query, key, value, grad_out, tile_start):
    groups = lax.axis_size("fsdp")
    position = lax.axis_index("fsdp")
    block_idx = lax.axis_index("ctx")
    seqs, rows, width = query.shape
    heads_here = HEADS // groups
    block_len = rows * groups
    even = position % 2 == 0
    paired = jnp.stack(
        [
            key.reshape(seqs, rows, KV_HEADS, HEAD_DIM),
            value.reshape(seqs, rows, KV_HEADS, HEAD_DIM),
        ],
        axis=3,
    )
    paired = paired.reshape(seqs, rows, 2 * KV_HEADS * HEAD_DIM)
    q_heads, g_heads, kv_heads = (
        lax.all_to_all(query, "fsdp", split_axis=2, concat_axis=1, tiled=True),
        lax.all_to_all(grad_out, "fsdp", split_axis=2, concat_axis=1, tiled=True),
        lax.all_to_all(paired, "fsdp", split_axis=2, concat_axis=1, tiled=True),
    )
    columns = kv_heads.shape[2]
    if columns >= 2 * HEAD_DIM:
        grouped = kv_heads.reshape(seqs, block_len, columns // (2 * HEAD_DIM), 2, HEAD_DIM)
        k_heads = jnp.repeat(grouped[:, :, :, 0], 2, axis=2)
        v_heads = jnp.repeat(grouped[:, :, :, 1], 2, axis=2)
    else:
        partner = partner_2(kv_heads, "fsdp", 0)
        k_heads = jnp.where(even, kv_heads, partner).reshape(seqs, block_len, 1, HEAD_DIM)
        v_heads = jnp.where(even, partner, kv_heads).reshape(seqs, block_len, 1, HEAD_DIM)
    q_heads = q_heads.reshape(seqs, block_len, heads_here, HEAD_DIM)
    g_heads = g_heads.reshape(seqs, block_len, heads_here, HEAD_DIM)
    earlier = passed_along(
        (k_heads[:, block_len - WINDOW :], v_heads[:, block_len - WINDOW :]), "ctx", 1
    )
    k_ext = jnp.concatenate([earlier[0], k_heads], axis=1)
    v_ext = jnp.concatenate([earlier[1], v_heads], axis=1)
    tiles_block = block_len // TILE
    tiles_here = lax.dynamic_slice_in_dim(tile_start, block_idx * tiles_block, tiles_block, 1)
    offset = block_idx * block_len
    span = QBLOCK + WINDOW
    per_seq = block_len // QBLOCK
    reach = span // QBLOCK
    pieces = (WINDOW + block_len) // QBLOCK
    seq_q, seq_k, seq_v = ([], [], [])
    for seq in range(seqs):
        parts_q, parts_k, parts_v = ([], [], [])
        for blk in range(per_seq):
            q0 = blk * QBLOCK
            q_blk = q_heads[seq, q0 : q0 + QBLOCK]
            g_blk = g_heads[seq, q0 : q0 + QBLOCK]
            k_span = k_ext[seq, q0 : q0 + span]
            v_span = v_ext[seq, q0 : q0 + span]
            first_tiles = tiles_here[seq, q0 // TILE : (q0 + QBLOCK) // TILE]
            starts = TILE * jnp.repeat(first_tiles, TILE)
            qpos = offset + q0 + jnp.arange(QBLOCK, dtype=jnp.int32)
            kpos = offset + q0 - WINDOW + jnp.arange(span, dtype=jnp.int32)
            visible = (
                (kpos[None, :] >= starts[:, None])
                & (kpos[None, :] <= qpos[:, None])
                & (qpos[:, None] - kpos[None, :] < WINDOW)
            )
            operands = (q_blk, g_blk, k_span, v_span, visible)
            bq, bk, bv = whole_span(operands)
            parts_q.append(bq)
            parts_k.append(bk)
            parts_v.append(bv)
        sums_k, sums_v = ([], [])
        for piece in range(pieces):
            total_k = None
            total_v = None
            for blk in range(max(0, piece - reach + 1), min(per_seq, piece + 1)):
                lower = (piece - blk) * QBLOCK
                term_k = parts_k[blk][lower : lower + QBLOCK]
                term_v = parts_v[blk][lower : lower + QBLOCK]
                total_k = term_k if total_k is None else total_k + term_k
                total_v = term_v if total_v is None else total_v + term_v
            sums_k.append(total_k)
            sums_v.append(total_v)
        seq_q.append(jnp.concatenate(parts_q, axis=0))
        seq_k.append(jnp.concatenate(sums_k, axis=0))
        seq_v.append(jnp.concatenate(sums_v, axis=0))
    grad_q = jnp.stack(seq_q)
    grad_k = jnp.stack(seq_k)
    grad_v = jnp.stack(seq_v)
    returned = (
        passed_along(grad_k[:, :WINDOW].astype(jnp.bfloat16), "ctx", -1).astype(jnp.float32),
        passed_along(grad_v[:, :WINDOW].astype(jnp.bfloat16), "ctx", -1).astype(jnp.float32),
    )
    head_k = grad_k[:, WINDOW:].at[:, block_len - WINDOW :].add(returned[0]).astype(jnp.bfloat16)
    head_v = grad_v[:, WINDOW:].at[:, block_len - WINDOW :].add(returned[1]).astype(jnp.bfloat16)
    flat_q = grad_q.reshape(seqs, block_len, heads_here * HEAD_DIM)
    if heads_here >= 2:
        sum_k = (
            head_k.reshape(seqs, block_len, heads_here // 2, 2, HEAD_DIM)
            .astype(jnp.float32)
            .sum(axis=3)
            .astype(jnp.bfloat16)
        )
        sum_v = (
            head_v.reshape(seqs, block_len, heads_here // 2, 2, HEAD_DIM)
            .astype(jnp.float32)
            .sum(axis=3)
            .astype(jnp.bfloat16)
        )
        summed = jnp.stack([sum_k, sum_v], axis=3).reshape(seqs, block_len, heads_here * HEAD_DIM)
    else:
        outgoing = jnp.where(even, head_v, head_k)
        incoming = partner_2(outgoing, "fsdp", 0)
        kept = jnp.where(even, head_k, head_v)
        summed = (
            (kept.astype(jnp.float32) + incoming.astype(jnp.float32))
            .astype(jnp.bfloat16)
            .reshape(seqs, block_len, HEAD_DIM)
        )
    rows_q, rows_kv = (
        lax.all_to_all(flat_q, "fsdp", split_axis=1, concat_axis=2, tiled=True),
        lax.all_to_all(summed, "fsdp", split_axis=1, concat_axis=2, tiled=True),
    )
    split = rows_kv.reshape(seqs, rows, KV_HEADS, 2, HEAD_DIM)
    out_k = split[:, :, :, 0]
    out_v = split[:, :, :, 1]
    return (
        rows_q,
        out_k.reshape(seqs, rows, KV_HEADS * HEAD_DIM),
        out_v.reshape(seqs, rows, KV_HEADS * HEAD_DIM),
    )


def solution(mesh):
    in_specs = (
        P(None, ("ctx", "fsdp"), None),
        P(None, ("ctx", "fsdp"), None),
        P(None, ("ctx", "fsdp"), None),
        P(None, ("ctx", "fsdp"), None),
        P(),
    )
    out_specs = (
        P(None, ("ctx", "fsdp"), None),
        P(None, ("ctx", "fsdp"), None),
        P(None, ("ctx", "fsdp"), None),
    )
    return jax.shard_map(body, mesh=mesh, in_specs=in_specs, out_specs=out_specs, check_vma=False)
```

profile of v0, /device:TPU:10, one launch (start us, length us, event | category | flops | bytes accessed | tf_op | source)
XLA Modules:
  0.0 979.5 jit_solution(14545384779352481896)
XLA Ops:
  9.4 27.2 %copy.119 = bf16[2,256,4096]{1,0,2:T(2,128)(2,1)} copy(bf16[2,256,4096]{1,2,0:T(8,128)(2,1)S(1)} %bitcast.620) | data formatting | bytes 8388608 | tf_op jit(solution)/shard_map/reshape | solution.py:71
  42.9 11.1 %copy.122 = bf16[2,256,4096]{1,0,2:T(2,128)(2,1)} copy(bf16[2,256,4096]{2,1,0:T(8,128)(2,1)} %param.9) | data formatting | bytes 8388608 | tf_op args[0]
  54.0 79.6 %all-to-all-done = bf16[2,256,4096]{1,0,2:T(2,128)(2,1)} async-done(((bf16[2,256,4096]{1,0,2:T(2,128)(2,1)}), bf16[2,256,4096]{1,0,2:T(2,128)(2,1)}, u32[]{:S(2)}, u32[]{:S(2)}) %all-to-all-start) | async-done | bytes 4194336 | tf_op jit(solution)/shard_map/all_to_all | solution.py:75
  140.6 11.1 %copy.126 = bf16[2,256,4096]{1,0,2:T(2,128)(2,1)} copy(bf16[2,256,4096]{2,1,0:T(8,128)(2,1)} %param.12) | data formatting | bytes 8388608 | tf_op args[3]
  151.8 78.9 %all-to-all-done.1 = bf16[2,256,4096]{1,0,2:T(2,128)(2,1)} async-done(((bf16[2,256,4096]{1,0,2:T(2,128)(2,1)}), bf16[2,256,4096]{1,0,2:T(2,128)(2,1)}, u32[]{:S(2)}, u32[]{:S(2)}) %all-to-all-start.1) | async-done | bytes 4194336 | tf_op jit(solution)/shard_map/all_to_all | solution.py:73
  342.0 12.1 %fusion.258 = (f32[4,512]{1,0:T(4,128)S(1)}, f32[4,512,1536]{1,2,0:T(8,128)S(1)}) fusion(f32[4,1536,512]{2,1,0:T(8,128)} %fusion.188, pred[512,1536]{0,1:T(8,128)(4,1)} %get-tuple-element.51), kind=kOutput, calls=%fused_computation.413 | output fusion | flops 18875904 | bytes 25960448 | tf_op jit(solution)/shard_map/sub | solution.py:34
  363.6 9.8 fusion.10
  379.4 14.0 %fusion.263 = (f32[4,512]{1,0:T(4,128)S(1)}, f32[4,512,1536]{1,2,0:T(8,128)}) fusion(f32[4,1536,512]{2,1,0:T(8,128)} %fusion.182, pred[512,1536]{0,1:T(8,128)(4,1)S(1)} %copy-done.48), kind=kOutput, calls=%fused_computation.418 | output fusion | flops 18875904 | bytes 25960448 | tf_op jit(solution)/shard_map/sub | solution.py:34
  410.0 9.6 fusion.35
  425.0 13.7 %fusion.262 = (f32[4,512]{1,0:T(4,128)S(1)}, f32[4,512,1536]{1,2,0:T(8,128)}) fusion(f32[4,1536,512]{2,1,0:T(8,128)} %fusion.184, pred[512,1536]{0,1:T(8,128)(4,1)S(1)} %get-tuple-element.50), kind=kOutput, calls=%fused_computation.417 | output fusion | flops 18875904 | bytes 25960448 | tf_op jit(solution)/shard_map/sub | solution.py:34
  455.6 9.6 fusion.30
  470.6 13.9 %fusion.259 = (f32[4,512]{1,0:T(4,128)S(1)}, f32[4,512,1536]{1,2,0:T(8,128)}) fusion(f32[4,1536,512]{2,1,0:T(8,128)} %fusion.186, pred[512,1536]{0,1:T(8,128)(4,1)S(1)} %copy-done.47), kind=kOutput, calls=%fused_computation.414 | output fusion | flops 18875904 | bytes 25960448 | tf_op jit(solution)/shard_map/sub | solution.py:34
  505.2 10.0 %fusion.15 = bf16[4,512,1536]{1,2,0:T(8,128)(2,1)S(1)} fusion(f32[4,1536,512]{2,1,0:T(8,128)} %get-tuple-element.67, f32[4,512]{1,0:T(4,128)S(1)} %get-tuple-element.66, f32[4,512,1536]{1,2,0:T(8,128)} %get-tuple-element.65, f32[4,512]{1,0:T(4,128)S(1)} %get-tuple-element.64), kind=kLoop, calls=%fused_computation.29 | loop fusion | flops 12582912 | bytes 31473664 | tf_op jit(solution)/shard_map/convert_element_type | solution.py:39
  528.7 22.6 %collective-permute-done = bf16[2,1024,4,128]{3,1,2,0:T(8,128)(2,1)S(1)} collective-permute-done((bf16[2,1024,4,128]{3,1,2,0:T(8,128)(2,1)S(1)}, bf16[2,1024,4,128]{3,1,2,0:T(8,128)(2,1)S(1)}, u32[]{:S(2)}, u32[]{:S(2)}) %collective-permute-start) | collective-permute-done | bytes 2097184 | tf_op jit(solution)/shard_map/ppermute | solution.py:26
  553.2 11.6 %fusion.261 = (f32[4,512]{1,0:T(4,128)S(1)}, f32[4,512,1536]{1,2,0:T(8,128)}) fusion(pred[512,1536]{0,1:T(8,128)(4,1)} %get-tuple-element.45, bf16[1536,4,128]{2,0,1:T(8,128)(2,1)} %get-tuple-element.39, bf16[2,2048,4,128]{1,3,2,0:T(8,128)(2,1)} %reshape.253), kind=kOutput, calls=%fused_computation.416 | convolution fusion | flops 1629488640 | bytes 18358272 | tf_op jit(solution)/shard_map/sub | solution.py:34
  595.9 9.5 fusion.260
  655.5 11.0 %fusion.264 = (f32[4,512]{1,0:T(4,128)S(1)}, f32[4,512,1536]{1,2,0:T(8,128)}) fusion(pred[512,1536]{0,1:T(8,128)(4,1)S(1)} %copy-done.45, bf16[1536,4,128]{2,0,1:T(8,128)(2,1)} %get-tuple-element.37, bf16[2,2048,4,128]{1,3,2,0:T(8,128)(2,1)} %reshape.253), kind=kOutput, calls=%fused_computation.419 | convolution fusion | flops 1629488640 | bytes 18358272 | tf_op jit(solution)/shard_map/sub | solution.py:34
  698.4 11.8 %fusion.38 = (f32[4,512]{1,0:T(4,128)S(1)}, f32[4,1536,512]{2,1,0:T(8,128)}) fusion(f32[4,512,1536]{1,2,0:T(8,128)} %get-tuple-element.85, f32[4,512]{1,0:T(4,128)S(1)} %get-tuple-element.84, bf16[2,2048,4,128]{1,3,2,0:T(8,128)(2,1)} %reshape.255, bf16[2,2048,4,128]{3,1,2,0:T(8,128)(2,1)} %bitcast.632, bf16[2,1024,4,128]{3,1,2,0:T(8,128)(2,1)} %collective-permute-done.1), kind=kOutput, calls=%fused_computation.72 | convolution fusion | flops 817887232 | bytes 31997952 | tf_op jit(solution)/shard_map/qhd,khd->hqk/dot_general | solution.py:37
  710.2 9.8 fusion.40
  748.8 10.8 %pad_maximum_fusion.3 = bf16[2,2048,512]{2,0,1:T(2,128)(2,1)} fusion(bf16[1,2048,512]{2,0,1:T(2,128)(2,1)} %copy.160, bf16[1,2048,512]{2,0,1:T(2,128)(2,1)} %copy.159), kind=kLoop, calls=%fused_computation.177 | loop fusion | flops 8388608 | bytes 8388608 | tf_op jit(solution)/shard_map/stack | solution.py:138
  805.0 11.7 %collective-permute-done.2 = bf16[2,1024,4,128]{3,1,2,0:T(8,128)(2,1)} collective-permute-done((bf16[2,1024,4,128]{3,1,2,0:T(8,128)(2,1)}, bf16[2,1024,4,128]{3,1,2,0:T(8,128)(2,1)}, u32[]{:S(2)}, u32[]{:S(2)}) %collective-permute-start.2) | collective-permute-done | bytes 2097184 | tf_op jit(solution)/shard_map/ppermute | solution.py:26
  836.7 11.1 %copy.163 = bf16[2,2048,512]{2,0,1:T(2,128)(2,1)} copy(bf16[2,2048,512]{1,2,0:T(8,128)(2,1)} %bitcast.624) | data formatting | bytes 8388608 | tf_op jit(solution)/shard_map/reshape | solution.py:161
  847.8 11.4 %all-to-all-done.3 = bf16[2,2048,512]{2,0,1:T(2,128)(2,1)} async-done(((bf16[2,2048,512]{2,0,1:T(2,128)(2,1)}), bf16[2,2048,512]{2,0,1:T(2,128)(2,1)}, u32[]{:S(2)}, u32[]{:S(2)}) %all-to-all-start.3) | async-done | bytes 4194336 | tf_op jit(solution)/shard_map/all_to_all | solution.py:172
  880.0 77.9 %all-to-all-done.4 = bf16[2,2048,512]{2,0,1:T(2,128)(2,1)} async-done(((bf16[2,2048,512]{2,0,1:T(2,128)(2,1)}), bf16[2,2048,512]{2,0,1:T(2,128)(2,1)}, u32[]{:S(2)}, u32[]{:S(2)}) %all-to-all-start.4) | async-done | bytes 4194336 | tf_op jit(solution)/shard_map/all_to_all | solution.py:173
  (275 shorter events, 477.7 us)
Async XLA Ops:
  0.6 237.4 %copy-start = (s32[2,64]{1,0:T(2,128)S(1)}, s32[2,64]{1,0:T(2,128)}, u32[]{:S(2)}) copy-start(s32[2,64]{1,0:T(2,128)} %param.13) | copy-start | bytes 1540
  36.6 97.0 %all-to-all-start = ((bf16[2,256,4096]{1,0,2:T(2,128)(2,1)}), bf16[2,256,4096]{1,0,2:T(2,128)(2,1)}, u32[]{:S(2)}, u32[]{:S(2)}) async-start(bf16[2,256,4096]{1,0,2:T(2,128)(2,1)} %copy.119), calls=%async_computation | async-start | bytes 8388608 | tf_op jit(solution)/shard_map/all_to_all | solution.py:75
  133.6 97.1 %all-to-all-start.1 = ((bf16[2,256,4096]{1,0,2:T(2,128)(2,1)}), bf16[2,256,4096]{1,0,2:T(2,128)(2,1)}, u32[]{:S(2)}, u32[]{:S(2)}) async-start(bf16[2,256,4096]{1,0,2:T(2,128)(2,1)} %copy.122), calls=%async_computation.1 | async-start | bytes 8388608 | tf_op jit(solution)/shard_map/all_to_all | solution.py:73
  230.7 97.3 %all-to-all-start.2 = ((bf16[2,256,4096]{1,0,2:T(2,128)(2,1)}), bf16[2,256,4096]{1,0,2:T(2,128)(2,1)}, u32[]{:S(2)}, u32[]{:S(2)}) async-start(bf16[2,256,4096]{1,0,2:T(2,128)(2,1)} %copy.126), calls=%async_computation.2 | async-start | bytes 8388608 | tf_op jit(solution)/shard_map/all_to_all | solution.py:74
  354.1 9.5 copy-start.18
  354.1 9.5 copy-start.49
  363.6 9.8 %copy-start.4 = (bf16[2,2048,2,2,128]{4,1,3,2,0:T(8,128)(2,1)S(1)}, bf16[2,2048,2,2,128]{4,1,3,2,0:T(8,128)(2,1)}, u32[]{:S(2)}) copy-start(bf16[2,2048,2,2,128]{4,1,3,2,0:T(8,128)(2,1)} %copy-done.2) | copy-start | bytes 12582916
  492.7 10.5 %copy-start.38 = (bf16[2,1024,4,128]{3,1,2,0:T(8,128)(2,1)S(1)}, bf16[2,1024,4,128]{3,1,2,0:T(8,128)(2,1)}, u32[]{:S(2)}) copy-start(bf16[2,1024,4,128]{3,1,2,0:T(8,128)(2,1)} %slice.457) | copy-start | bytes 6291460
  501.3 71.7 %collective-permute-start.1 = (bf16[2,1024,4,128]{3,1,2,0:T(8,128)(2,1)}, bf16[2,1024,4,128]{3,1,2,0:T(8,128)(2,1)}, u32[]{:S(2)}, u32[]{:S(2)}) collective-permute-start(bf16[2,1024,4,128]{3,1,2,0:T(8,128)(2,1)} %slice.462), channel_id=1, source_target_pairs={{0,8},{8,16},{16,24},{1,9},{9,17},{17,25},{2,10},{10,18},{18,26},{... | collective-permute-start | bytes 6291464 | tf_op jit(solution)/shard_map/ppermute | solution.py:26
  503.3 48.1 %collective-permute-start = (bf16[2,1024,4,128]{3,1,2,0:T(8,128)(2,1)S(1)}, bf16[2,1024,4,128]{3,1,2,0:T(8,128)(2,1)S(1)}, u32[]{:S(2)}, u32[]{:S(2)}) collective-permute-start(bf16[2,1024,4,128]{3,1,2,0:T(8,128)(2,1)S(1)} %copy-done.38), channel_id=1, source_target_pairs={{0,8},{8,16},{16,24},{1,9},{9,17},{17,25},{2,10},{10,18},{18,26},{... | collective-permute-start | bytes 6291464 | tf_op jit(solution)/shard_map/ppermute | solution.py:26
  553.2 82.8 %copy-start.26 = (bf16[1536,4,128]{2,0,1:T(8,128)(2,1)}, bf16[1536,4,128]{2,0,1:T(8,128)(2,1)S(1)}, u32[]{:S(2)}) copy-start(bf16[1536,4,128]{2,0,1:T(8,128)(2,1)S(1)} %get-tuple-element.36) | copy-start | bytes 4718596
  564.8 9.4 copy-start.19
  564.8 10.6 %copy-start.23 = (bf16[2,2048,2,2,128]{4,1,3,2,0:T(8,128)(2,1)S(1)}, bf16[2,2048,2,2,128]{4,1,3,2,0:T(8,128)(2,1)}, u32[]{:S(2)}) copy-start(bf16[2,2048,2,2,128]{4,1,3,2,0:T(8,128)(2,1)} %copy-done.21) | copy-start | bytes 12582916
  605.4 9.4 copy-start.20
  605.4 10.6 %copy-start.24 = (bf16[2,2048,2,2,128]{4,1,3,2,0:T(8,128)(2,1)S(1)}, bf16[2,2048,2,2,128]{4,1,3,2,0:T(8,128)(2,1)}, u32[]{:S(2)}) copy-start(bf16[2,2048,2,2,128]{4,1,3,2,0:T(8,128)(2,1)} %copy-done.21) | copy-start | bytes 12582916
  655.5 17.6 %slice-start.10 = ((s8[6291456]{0:T(1024)(128)(4,1)}), s8[2097152]{0:T(1024)(128)(4,1)S(1)}, s32[]{:S(2)}) async-start(s8[6291456]{0:T(1024)(128)(4,1)} %bitcast.609), calls=%async_computation.15 | async-start | bytes 4194304
  686.2 111.3 %collective-permute-start.3 = (bf16[2,1024,4,128]{3,1,2,0:T(8,128)(2,1)}, bf16[2,1024,4,128]{3,1,2,0:T(8,128)(2,1)}, u32[]{:S(2)}, u32[]{:S(2)}) collective-permute-start(bf16[2,1024,4,128]{3,1,2,0:T(8,128)(2,1)} %fusion.112), channel_id=1, source_target_pairs={{8,0},{16,8},{24,16},{9,1},{17,9},{25,17},{10,2},{18,10},{26,18},{... | collective-permute-start | bytes 6291464 | tf_op jit(solution)/shard_map/ppermute | solution.py:26
  698.4 25.3 %slice-start.14 = ((s8[12582912]{0:T(1024)(128)(4,1)}), s8[4194304]{0:T(1024)(128)(4,1)S(1)}, s32[]{:S(2)}) async-start(s8[12582912]{0:T(1024)(128)(4,1)} %bitcast.628), calls=%async_computation.19 | async-start | bytes 8388608
  698.4 25.3 %slice-start.15 = ((s8[12582912]{0:T(1024)(128)(4,1)}), s8[4194304]{0:T(1024)(128)(4,1)S(1)}, s32[]{:S(2)}) async-start(s8[12582912]{0:T(1024)(128)(4,1)} %bitcast.628), calls=%async_computation.20 | async-start | bytes 8388608
  710.2 12.4 %copy-start.28 = (bf16[1536,4,128]{2,0,1:T(8,128)(2,1)S(1)}, bf16[1536,4,128]{2,0,1:T(8,128)(2,1)}, u32[]{:S(2)}) copy-start(bf16[1536,4,128]{2,0,1:T(8,128)(2,1)} %get-tuple-element.37) | copy-start | bytes 4718596
  710.2 13.5 %slice-start.16 = ((s8[12582912]{0:T(1024)(128)(4,1)}), s8[4194304]{0:T(1024)(128)(4,1)S(1)}, s32[]{:S(2)}) async-start(s8[12582912]{0:T(1024)(128)(4,1)} %bitcast.628), calls=%async_computation.21 | async-start | bytes 8388608
  759.6 99.6 %all-to-all-start.3 = ((bf16[2,2048,512]{2,0,1:T(2,128)(2,1)}), bf16[2,2048,512]{2,0,1:T(2,128)(2,1)}, u32[]{:S(2)}, u32[]{:S(2)}) async-start(bf16[2,2048,512]{2,0,1:T(2,128)(2,1)} %pad_maximum_fusion.3), calls=%async_computation.3 | async-start | bytes 8388608 | tf_op jit(solution)/shard_map/all_to_all | solution.py:172
  790.6 26.2 %collective-permute-start.2 = (bf16[2,1024,4,128]{3,1,2,0:T(8,128)(2,1)}, bf16[2,1024,4,128]{3,1,2,0:T(8,128)(2,1)}, u32[]{:S(2)}, u32[]{:S(2)}) collective-permute-start(bf16[2,1024,4,128]{3,1,2,0:T(8,128)(2,1)} %fusion.113), channel_id=1, source_target_pairs={{8,0},{16,8},{24,16},{9,1},{17,9},{25,17},{10,2},{18,10},{26,18},{... | collective-permute-start | bytes 6291464 | tf_op jit(solution)/shard_map/ppermute | solution.py:26
  859.2 98.7 %all-to-all-start.4 = ((bf16[2,2048,512]{2,0,1:T(2,128)(2,1)}), bf16[2,2048,512]{2,0,1:T(2,128)(2,1)}, u32[]{:S(2)}, u32[]{:S(2)}) async-start(bf16[2,2048,512]{2,0,1:T(2,128)(2,1)} %copy.163), calls=%async_computation.4 | async-start | bytes 8388608 | tf_op jit(solution)/shard_map/all_to_all | solution.py:173
  (53 other events, 255.4 us)
where the time goes:
time: 989 us; the launch traced here: 979 us
  waiting for transfers between devices  288 us (29%)
  matrix products  244 us (25%)
  local copies, waits for them, and re-layouts  219 us (22%)
  other arithmetic  184 us (19%)
  starting transfers between devices  43.1 us (4%)
    all_to_all x1, waiting for transfers between devices, body(): lax.all_to_all(paired, 'fsdp', split_axis=2, concat_axis=1, tiled=True)  79.6 us
    all_to_all x1, waiting for transfers between devices, body(): lax.all_to_all(query, 'fsdp', split_axis=2, concat_axis=1, tiled=True)  78.9 us
    all_to_all x1, waiting for transfers between devices, body(): lax.all_to_all(summed, 'fsdp', split_axis=1, concat_axis=2, tiled=True)  77.9 us
    unnamed x146, local copies, waits for them, and re-layouts  71.5 us
    dot_general x8, matrix products, block_grads(): jnp.einsum('qhd,khd->hqk', g_blk, v_span, preferred_element_type=jnp.floa...  70 us
    convert_element_type x8, other arithmetic, block_grads(): grad_scores = (probs * (grad_probs - delta)).astype(jnp.bfloat16)  66.7 us
    dot_general x8, matrix products, block_grads(): jnp.einsum('hqk,qhd->khd', probs_low, g_blk, preferred_element_type=jnp.f...  62.1 us
    sub x4, other arithmetic, block_grads(): weights = jnp.exp(jnp.where(visible, scores - top, -jnp.inf))  53.7 us
  transfers between devices with their start and end apart: 9, of which 7 were waited for; matrix products, arithmetic and copies ran while one was open for 29% of the time, Pallas kernels for 0%

commit v1 on v0

v1 whole, which is shorter than its diff:
```python
import math

import jax
import jax.numpy as jnp
from jax import lax
from jax.experimental import pallas as pl
from jax.experimental.pallas import tpu as pltpu
from jax.sharding import PartitionSpec as P

HEADS = 32
KV_HEADS = 16
HEAD_DIM = 128
WINDOW = 1024
TILE = 128
BLOCK = 512
HALF = 256
HEAD_GROUPS = 2

score_scale = 168.0 ** (-0.5)
exp2_scale = score_scale * math.log2(math.e)

VMEM_LIMIT = 48 * 1024 * 1024


def attention_kernel(starts, qg_ref, kv0, kv1, kv2, dq_ref, d0, d1, d2, kt_s, dk_s, dv_s):
    span = [(kv2, 0), (kv2, HALF), (kv1, 0), (kv1, HALF), (kv0, 0), (kv0, HALF)]
    pieces = len(span)
    for n, (ref, lower) in enumerate(span):
        kt_s[n] = ref[0, lower : lower + HALF, :].T
    dk_s[...] = jnp.zeros_like(dk_s)
    dv_s[...] = jnp.zeros_like(dv_s)
    lane = lax.broadcasted_iota(jnp.int32, (1, HALF), 1)
    k_iota = lax.broadcasted_iota(jnp.int32, (HALF, HALF), 0)
    tiles = HALF // TILE
    for j in range(BLOCK // HALF):
        begin = starts[tiles * j]
        first = jnp.full((1, HALF), begin, jnp.int32)
        for t in range(1, tiles):
            first = jnp.where(lane >= t * TILE, starts[tiles * j + t], first)
        q_pos = WINDOW + j * HALF + lane
        count = WINDOW // HALF + 1
        for head in range(2):
            cols = slice(head * HEAD_DIM, (head + 1) * HEAD_DIM)
            rows = slice(j * HALF, (j + 1) * HALF)
            q = qg_ref[0, rows, cols]
            g = qg_ref[1, rows, cols]
            scores = []
            top = None
            for i in range(count):
                ref, lower = span[j + i]
                k = ref[0, lower : lower + HALF, :]
                s = lax.dot_general(
                    k, q, (((1,), (1,)), ((), ())), preferred_element_type=jnp.float32
                )
                k_pos = (j + i) * HALF + k_iota
                visible = k_pos >= first
                if i == 0:
                    visible = visible & (k_pos > q_pos - WINDOW)
                if i == count - 1:
                    visible = visible & (k_pos <= q_pos)
                s = jnp.where(visible, s, -jnp.inf)
                peak = jnp.max(s, axis=0, keepdims=True)
                top = peak if top is None else jnp.maximum(top, peak)
                scores.append(s)
            shift = top * exp2_scale
            weights, grads = [], []
            total, inner = None, None
            for i in range(count):
                ref, lower = span[j + i]
                v = ref[1, lower : lower + HALF, :]
                w = jnp.exp2(scores[i] * exp2_scale - shift)
                dp = lax.dot_general(
                    v, g, (((1,), (1,)), ((), ())), preferred_element_type=jnp.float32
                )
                part = jnp.sum(w, axis=0, keepdims=True)
                mixed = jnp.sum(w * dp, axis=0, keepdims=True)
                total = part if total is None else total + part
                inner = mixed if inner is None else inner + mixed
                weights.append(w)
                grads.append(dp)
            inverse = 1.0 / total
            delta = inner * inverse
            dq_t = None
            for i in range(count):
                at = slice((j + i) * HALF, (j + i + 1) * HALF)
                probs = weights[i] * inverse
                ds = (probs * (grads[i] - delta)).astype(jnp.bfloat16)
                low = probs.astype(jnp.bfloat16)
                dv_s[at, :] += jnp.dot(low, g, preferred_element_type=jnp.float32)
                dk_s[at, :] += jnp.dot(ds, q, preferred_element_type=jnp.float32)
                term = jnp.dot(kt_s[j + i], ds, preferred_element_type=jnp.float32)
                dq_t = term if dq_t is None else dq_t + term
            dq_ref[rows, cols] = (dq_t.T * score_scale).astype(jnp.bfloat16)
    for n, out in enumerate((d2, d1, d0)):
        at = slice(n * BLOCK, (n + 1) * BLOCK)
        out[0] = (dk_s[at, :] * score_scale).astype(jnp.bfloat16)
        out[1] = dv_s[at, :].astype(jnp.bfloat16)


def attention(starts, qg, kv0, kv1, kv2):
    kv_heads = kv0.shape[2] // HEAD_DIM
    both = pl.BlockSpec((2, BLOCK, 2 * HEAD_DIM), lambda h, *_: (0, 0, h))
    wide = pl.BlockSpec((BLOCK, 2 * HEAD_DIM), lambda h, *_: (0, h))
    pair = pl.BlockSpec((2, BLOCK, HEAD_DIM), lambda h, *_: (0, 0, h))
    pair_shape = jax.ShapeDtypeStruct(kv0.shape, jnp.bfloat16)
    keys = WINDOW + BLOCK
    work = kv_heads * 2 * BLOCK * (WINDOW + HALF)
    return pl.pallas_call(
        attention_kernel,
        grid_spec=pltpu.PrefetchScalarGridSpec(
            num_scalar_prefetch=1,
            grid=(kv_heads,),
            in_specs=[both, pair, pair, pair],
            out_specs=[wide, pair, pair, pair],
            scratch_shapes=[
                pltpu.VMEM((keys // HALF, HEAD_DIM, HALF), jnp.bfloat16),
                pltpu.VMEM((keys, HEAD_DIM), jnp.float32),
                pltpu.VMEM((keys, HEAD_DIM), jnp.float32),
            ],
        ),
        out_shape=[jax.ShapeDtypeStruct(qg.shape[1:], jnp.bfloat16)] + [pair_shape] * 3,
        compiler_params=pltpu.CompilerParams(vmem_limit_bytes=VMEM_LIMIT),
        cost_estimate=pl.CostEstimate(
            flops=20 * work * HEAD_DIM, bytes_accessed=8 * qg.size, transcendentals=work
        ),
        name="attention",
    )(starts, qg, kv0, kv1, kv2)


def call_copies(kernel, part, operands, in_specs, out_specs, out_shape, grid=(1,), aliases=None):
    moved = sum(math.prod(shape.shape) for shape in out_shape)
    return pl.pallas_call(
        kernel,
        grid_spec=pltpu.PrefetchScalarGridSpec(
            num_scalar_prefetch=1, grid=grid, in_specs=in_specs, out_specs=out_specs
        ),
        out_shape=out_shape,
        input_output_aliases=aliases or {},
        compiler_params=pltpu.CompilerParams(vmem_limit_bytes=VMEM_LIMIT),
        cost_estimate=pl.CostEstimate(flops=0, bytes_accessed=4 * moved, transcendentals=0),
        name="copies",
    )(part, *operands)


def pack(part, arrays, seq, group):
    rows, width = arrays[0].shape[1], arrays[0].shape[2]
    cols = width // (2 * HEAD_GROUPS)
    count = len(arrays)

    def kernel(_, *refs):
        for n in range(count):
            refs[count][n] = refs[n][0]

    block = pl.BlockSpec((1, rows, cols), lambda _, y: (seq, 0, (1 - y[0]) * HEAD_GROUPS + group))
    shape = (count, rows, cols)
    return call_copies(
        kernel,
        part,
        arrays,
        [block] * count,
        [pl.BlockSpec(shape, lambda *_: (0, 0, 0))],
        [jax.ShapeDtypeStruct(shape, jnp.bfloat16)],
    )[0]


def assemble(part, arrays, came, seq, group):
    rows, width = arrays[0].shape[1], arrays[0].shape[2]
    cols = width // (2 * HEAD_GROUPS)
    count = len(arrays)

    def kernel(part_ref, *refs):
        out = refs[count + 1]
        here = pl.multiple_of(part_ref[0] * rows, rows)
        there = pl.multiple_of((1 - part_ref[0]) * rows, rows)
        for n in range(count):
            out[n, pl.ds(here, rows), :] = refs[n][0]
            out[n, pl.ds(there, rows), :] = refs[count][n]

    block = pl.BlockSpec((1, rows, cols), lambda _, y: (seq, 0, y[0] * HEAD_GROUPS + group))
    shape = (count, 2 * rows, cols)
    return call_copies(
        kernel,
        part,
        list(arrays) + [came],
        [block] * count + [pl.BlockSpec(came.shape, lambda *_: (0, 0, 0))],
        [pl.BlockSpec(shape, lambda *_: (0, 0, 0))],
        [jax.ShapeDtypeStruct(shape, jnp.bfloat16)],
    )[0]


def place(part, kept, came, outs, shape, seq, group):
    count, rows, cols = kept.shape
    old = [] if outs is None else list(outs)

    def kernel(_, kept_ref, came_ref, *refs):
        results = refs[len(old) :]

        @pl.when(pl.program_id(0) == 0)
        def _():
            for n in range(count):
                results[n][0] = kept_ref[n]

        @pl.when(pl.program_id(0) == 1)
        def _():
            for n in range(count):
                results[n][0] = came_ref[n]

    whole = pl.BlockSpec(kept.shape, lambda *_: (0, 0, 0))
    block = pl.BlockSpec(
        (1, rows, cols),
        lambda i, y: (seq, 0, (y[0] + i - 2 * i * y[0]) * HEAD_GROUPS + group),
    )
    return call_copies(
        kernel,
        part,
        [kept, came] + old,
        [whole, whole] + [pl.BlockSpec(memory_space=pl.ANY)] * len(old),
        [block] * count,
        [jax.ShapeDtypeStruct(shape, jnp.bfloat16)] * count,
        grid=(2,),
        aliases={3 + n: n for n in range(len(old))},
    )


def swapped(value):
    pairs = [(i, i ^ 1) for i in range(lax.axis_size("fsdp"))]
    return lax.ppermute(value, "fsdp", pairs)


def shifted(value, by):
    count = lax.axis_size("ctx") * lax.axis_size("fsdp")
    pairs = [(i, i + by) for i in range(count) if 0 <= i + by < count]
    return lax.ppermute(value, ("ctx", "fsdp"), pairs)


def pair_groups(split):
    groups = lax.axis_size("fsdp")
    return [list(range(n, n + split)) for n in range(0, groups, split)]


def to_heads(part, arrays, seq, group, split):
    if split == 2:
        came = swapped(pack(part, arrays, seq, group))
        return assemble(part, arrays, came, seq, group)
    rows, width = arrays[0].shape[1], arrays[0].shape[2]
    cols = width // split // HEAD_GROUPS
    stacked = jnp.stack(
        [a[seq].reshape(rows, split, HEAD_GROUPS, cols)[:, :, group] for a in arrays]
    )
    whole = lax.all_to_all(
        stacked, "fsdp", 2, 1, axis_index_groups=pair_groups(split), tiled=True
    )
    return whole.reshape(len(arrays), split * rows, cols)


def to_tokens(part, block, outs, shape, seq, group, split):
    count, length, cols = block.shape
    rows = length // split
    if split == 2:
        here = part[0]
        send = lax.dynamic_slice_in_dim(block, (1 - here) * rows, rows, 1)
        kept = lax.dynamic_slice_in_dim(block, here * rows, rows, 1)
        return place(part, kept, swapped(send), outs, shape, seq, group)
    if outs is None:
        outs = [jnp.zeros(shape, jnp.bfloat16)] * count
    parts = block.reshape(count, split, rows, cols)
    whole = lax.all_to_all(parts, "fsdp", 1, 1, axis_index_groups=pair_groups(split), tiled=True)
    results = []
    for n in range(count):
        result = outs[n]
        for p in range(split):
            left = (p * HEAD_GROUPS + group) * cols
            result = lax.dynamic_update_slice(result, whole[n, p][None], (seq, 0, left))
        results.append(result)
    return results


def added(one, other):
    return (one.astype(jnp.float32) + other.astype(jnp.float32)).astype(jnp.bfloat16)


def body(query, key, value, grad_out, tile_start):
    seqs, rows, _ = query.shape
    split = BLOCK // rows
    position = lax.axis_index("fsdp")
    part = jnp.full((1,), position % split, jnp.int32)
    blocks = lax.axis_size("fsdp") // split
    block = lax.axis_index("ctx") * blocks + position // split
    per_block = BLOCK // TILE
    tiles = lax.dynamic_slice_in_dim(tile_start, block * per_block, per_block, 1)
    starts = tiles * TILE - (block * BLOCK - WINDOW)
    chunks = [(s, h) for s in range(seqs) for h in range(HEAD_GROUPS)]
    inputs = []
    for seq, group in chunks:
        kv = to_heads(part, (key, value), seq, group, split)
        qg = to_heads(part, (query, grad_out), seq, group, split)
        inputs.append((kv, qg))
    outs_q, outs_kv = None, None
    for (seq, group), (kv0, qg) in zip(chunks, inputs):
        kv1 = shifted(kv0, split)
        kv2 = shifted(kv1, split)
        dq, d0, d1, d2 = attention(starts[seq], qg, kv0, kv1, kv2)
        outs_q = to_tokens(part, dq[None], outs_q, query.shape, seq, group, split)
        back = added(d1, shifted(d2, -split))
        total = added(d0, shifted(back, -split))
        outs_kv = to_tokens(part, total, outs_kv, key.shape, seq, group, split)
    return outs_q[0], outs_kv[0], outs_kv[1]


def solution(mesh):
    tokens = P(None, ("ctx", "fsdp"), None)
    return jax.shard_map(
        body,
        mesh=mesh,
        in_specs=(tokens, tokens, tokens, tokens, P()),
        out_specs=(tokens, tokens, tokens),
        check_vma=False,
    )
```

time: 989 us -> 560 us (0.57)
  matrix products: 244 us -> 0 us
  local copies, waits for them, and re-layouts: 219 us -> 13.8 us
  other arithmetic: 184 us -> 6.22 us
  Pallas kernels: 0 us -> 125 us
  waiting for transfers between devices: 288 us -> 336 us
  starting transfers between devices: 43.1 us -> 75.8 us
    ppermute x4 -> x32, waiting for transfers between devices: 34.3 us -> 336 us  [the longest x16 217 us: shifted(): return lax.ppermute(value, ('ctx', 'fsdp'), pairs)]
    all_to_all x5 -> x0, waiting for transfers between devices: 253 us -> none  [the longest x1 79.6 us: body(): lax.all_to_all(paired, 'fsdp', split_axis=2, concat_axis=1, tiled=True)]
    dot_general x36 -> x0, matrix products: 203 us -> none  [the longest x8 70 us: block_grads(): jnp.einsum('qhd,khd->hqk', g_blk, v_span, preferred_element_type=jnp.floa...]
    pallas_call x0 -> x28, Pallas kernels: none -> 125 us  [the longest x4 96 us: attention(): pl.pallas_call(attention_kernel, grid_spec=pltpu.PrefetchScalarGridSpec(n...]
    ppermute x4 -> x32, starting transfers between devices: 8.06 us -> 75.8 us  [the longest x16 57.9 us: shifted(): return lax.ppermute(value, ('ctx', 'fsdp'), pairs)]
    reshape x5 -> x0, local copies, waits for them, and re-layouts: 60.7 us -> none  [the longest x1 27.2 us: body(): paired = paired.reshape(seqs, rows, 2 * KV_HEADS * HEAD_DIM)]
    convert_element_type x8, other arithmetic: 66.7 us -> 6.14 us  [added(): (one.astype(jnp.float32) + other.astype(jnp.float32)).astype(jnp.bfloat16)]
    unnamed x146 -> x26, local copies, waits for them, and re-layouts: 71.5 us -> 13.2 us
  transfers between devices with their start and end apart: 9 -> 32, of which waited for: 7 -> 18; matrix products, arithmetic and copies ran while one was open for 29% -> 1% of each run, Pallas kernels for 0% -> 22%
where the time goes in v1:
time: 560 us; the launch traced here: 559 us
  waiting for transfers between devices  336 us (60%)
  Pallas kernels  125 us (22%)
  starting transfers between devices  75.8 us (14%)
  local copies, waits for them, and re-layouts  13.8 us (2%)
  other arithmetic  6.22 us (1%)
    ppermute x16, waiting for transfers between devices, shifted(): return lax.ppermute(value, ('ctx', 'fsdp'), pairs)  217 us
    ppermute x16, waiting for transfers between devices, swapped(): return lax.ppermute(value, 'fsdp', pairs)  120 us
    pallas_call x4, Pallas kernels, attention(): pl.pallas_call(attention_kernel, grid_spec=pltpu.PrefetchScalarGridSpec(n...  96 us
    ppermute x16, starting transfers between devices, shifted(): return lax.ppermute(value, ('ctx', 'fsdp'), pairs)  57.9 us
    pallas_call x24, Pallas kernels, call_copies(): pl.pallas_call(kernel, grid_spec=pltpu.PrefetchScalarGridSpec(num_scalar_...  29.2 us
    ppermute x16, starting transfers between devices, swapped(): return lax.ppermute(value, 'fsdp', pairs)  17.9 us
    unnamed x26, local copies, waits for them, and re-layouts  13.2 us
  transfers between devices with their start and end apart: 32, of which 18 were waited for; matrix products, arithmetic and copies ran while one was open for 1% of the time, Pallas kernels for 22%

profile of v1, /device:TPU:10, one launch (start us, length us, event | category | flops | bytes accessed | tf_op | source)
XLA Modules:
  0.0 558.6 jit_solution(11962330645856134129)
XLA Ops:
  14.7 4.0 collective-permute-done.16.refs_2_
  23.1 6.9 %collective-permute-done.11.refs_2_ = bf16[2,256,512]{2,1,0:T(8,128)(2,1)} collective-permute-done((bf16[2,256,512]{2,1,0:T(8,128)(2,1)}, bf16[2,256,512]{2,1,0:T(8,128)(2,1)}, u32[]{:S(2)}, u32[]{:S(2)}) %collective-permute-start.11) | collective-permute-done | bytes 524320 | tf_op jit(solution)/shard_map/ppermute | solution.py:227
  34.4 6.9 %collective-permute-done.6.refs_2_ = bf16[2,256,512]{2,1,0:T(8,128)(2,1)} collective-permute-done((bf16[2,256,512]{2,1,0:T(8,128)(2,1)}, bf16[2,256,512]{2,1,0:T(8,128)(2,1)}, u32[]{:S(2)}, u32[]{:S(2)}) %collective-permute-start.6) | collective-permute-done | bytes 524320 | tf_op jit(solution)/shard_map/ppermute | solution.py:227
  49.2 69.6 %collective-permute-done.1.refs_2_ = bf16[2,256,512]{2,1,0:T(8,128)(2,1)} collective-permute-done((bf16[2,256,512]{2,1,0:T(8,128)(2,1)}, bf16[2,256,512]{2,1,0:T(8,128)(2,1)}, u32[]{:S(2)}, u32[]{:S(2)}) %collective-permute-start.1) | collective-permute-done | bytes 524320 | tf_op jit(solution)/shard_map/ppermute | solution.py:227
  146.2 4.6 collective-permute-done.12.kv1
  154.2 19.0 %collective-permute-done.7.kv1 = bf16[2,512,512]{2,1,0:T(8,128)(2,1)} collective-permute-done((bf16[2,512,512]{2,1,0:T(8,128)(2,1)}, bf16[2,512,512]{2,1,0:T(8,128)(2,1)}, u32[]{:S(2)}, u32[]{:S(2)}) %collective-permute-start.7) | collective-permute-done | bytes 1048608 | tf_op jit(solution)/shard_map/ppermute | solution.py:233
  176.7 19.0 %collective-permute-done.2.kv1 = bf16[2,512,512]{2,1,0:T(8,128)(2,1)} collective-permute-done((bf16[2,512,512]{2,1,0:T(8,128)(2,1)}, bf16[2,512,512]{2,1,0:T(8,128)(2,1)}, u32[]{:S(2)}, u32[]{:S(2)}) %collective-permute-start.2) | collective-permute-done | bytes 1048608 | tf_op jit(solution)/shard_map/ppermute | solution.py:233
  199.2 19.0 %collective-permute-done.18.kv2 = bf16[2,512,512]{2,1,0:T(8,128)(2,1)} collective-permute-done((bf16[2,512,512]{2,1,0:T(8,128)(2,1)}, bf16[2,512,512]{2,1,0:T(8,128)(2,1)}, u32[]{:S(2)}, u32[]{:S(2)}) %collective-permute-start.18) | collective-permute-done | bytes 1048608 | tf_op jit(solution)/shard_map/ppermute | solution.py:233
  218.2 24.0 %attention.7 = (bf16[512,1024]{1,0:T(8,128)(2,1)S(1)}, bf16[2,512,512]{2,1,0:T(8,128)(2,1)S(1)}, bf16[2,512,512]{2,1,0:T(8,128)(2,1)S(1)}, bf16[2,512,512]{2,1,0:T(8,128)(2,1)}) custom-call(s32[4]{0:T(128)S(1)} %get-tuple-element.67.starts, bf16[2,512,1024]{2,1,0:T(8,128)(2,1)} %copy-done.6, bf16[2,512,512]{2,1,0:T(8,128)(2,1)} %copies.39.kv0, ...), custom_call_target="tpu_custom_call" | custom-call | flops 13421772800 | bytes 8388608 | tf_op jit(solution)/shard_map/attention/pallas_call | solution.py:108
  242.2 4.5 collective-permute-start.29
  247.7 24.0 %attention.6 = (bf16[512,1024]{1,0:T(8,128)(2,1)S(1)}, bf16[2,512,512]{2,1,0:T(8,128)(2,1)S(1)}, bf16[2,512,512]{2,1,0:T(8,128)(2,1)S(1)}, bf16[2,512,512]{2,1,0:T(8,128)(2,1)}) custom-call(s32[4]{0:T(128)S(1)} %get-tuple-element.67.starts, bf16[2,512,1024]{2,1,0:T(8,128)(2,1)} %copy-done.5, bf16[2,512,512]{2,1,0:T(8,128)(2,1)} %copies.35.kv0, ...), custom_call_target="tpu_custom_call" | custom-call | flops 13421772800 | bytes 8388608 | tf_op jit(solution)/shard_map/attention/pallas_call | solution.py:108
  274.6 24.0 %attention.5 = (bf16[512,1024]{1,0:T(8,128)(2,1)S(1)}, bf16[2,512,512]{2,1,0:T(8,128)(2,1)S(1)}, bf16[2,512,512]{2,1,0:T(8,128)(2,1)S(1)}, bf16[2,512,512]{2,1,0:T(8,128)(2,1)}) custom-call(s32[4]{0:T(128)S(1)} %get-tuple-element.68.starts, bf16[2,512,1024]{2,1,0:T(8,128)(2,1)} %copy-done.4, bf16[2,512,512]{2,1,0:T(8,128)(2,1)} %copies.31.kv0, ...), custom_call_target="tpu_custom_call" | custom-call | flops 13421772800 | bytes 8388608 | tf_op jit(solution)/shard_map/attention/pallas_call | solution.py:108
  301.7 24.0 %attention.4 = (bf16[512,1024]{1,0:T(8,128)(2,1)S(1)}, bf16[2,512,512]{2,1,0:T(8,128)(2,1)S(1)}, bf16[2,512,512]{2,1,0:T(8,128)(2,1)S(1)}, bf16[2,512,512]{2,1,0:T(8,128)(2,1)}) custom-call(s32[4]{0:T(128)S(1)} %get-tuple-element.68.starts, bf16[2,512,1024]{2,1,0:T(8,128)(2,1)} %copy-done.3, bf16[2,512,512]{2,1,0:T(8,128)(2,1)} %copies.27.kv0, ...), custom_call_target="tpu_custom_call" | custom-call | flops 13421772800 | bytes 8388608 | tf_op jit(solution)/shard_map/attention/pallas_call | solution.py:108
  330.0 4.4 collective-permute-start.30
  337.6 14.5 %collective-permute-start.27 = (bf16[2,512,512]{2,1,0:T(8,128)(2,1)S(1)}, bf16[2,512,512]{2,1,0:T(8,128)(2,1)S(1)}, u32[]{:S(2)}, u32[]{:S(2)}) collective-permute-start(bf16[2,512,512]{2,1,0:T(8,128)(2,1)S(1)} %add_convert_fusion.3), channel_id=1, source_target_pairs={{2,0},{3,1},{4,2},{5,3},{6,4},{7,5},{8,6},{9,7},{10,8},{11,9},{12,... | collective-permute-start | bytes 3145736 | tf_op jit(solution)/shard_map/ppermute | solution.py:233
  353.7 83.2 %collective-permute-done.20 = bf16[2,512,512]{2,1,0:T(8,128)(2,1)S(1)} collective-permute-done((bf16[2,512,512]{2,1,0:T(8,128)(2,1)}, bf16[2,512,512]{2,1,0:T(8,128)(2,1)S(1)}, u32[]{:S(2)}, u32[]{:S(2)}) %collective-permute-start.20) | collective-permute-done | bytes 1048608 | tf_op jit(solution)/shard_map/ppermute | solution.py:233
  439.1 19.4 %collective-permute-done.30 = bf16[2,512,512]{2,1,0:T(8,128)(2,1)S(1)} collective-permute-done((bf16[2,512,512]{2,1,0:T(8,128)(2,1)S(1)}, bf16[2,512,512]{2,1,0:T(8,128)(2,1)S(1)}, u32[]{:S(2)}, u32[]{:S(2)}) %collective-permute-start.30) | collective-permute-done | bytes 1048608 | tf_op jit(solution)/shard_map/ppermute | solution.py:233
  460.8 20.1 %collective-permute-done.27 = bf16[2,512,512]{2,1,0:T(8,128)(2,1)S(1)} collective-permute-done((bf16[2,512,512]{2,1,0:T(8,128)(2,1)S(1)}, bf16[2,512,512]{2,1,0:T(8,128)(2,1)S(1)}, u32[]{:S(2)}, u32[]{:S(2)}) %collective-permute-start.27) | collective-permute-done | bytes 1048608 | tf_op jit(solution)/shard_map/ppermute | solution.py:233
  481.9 21.6 %collective-permute-done.24 = bf16[2,512,512]{2,1,0:T(8,128)(2,1)S(1)} collective-permute-done((bf16[2,512,512]{2,1,0:T(8,128)(2,1)S(1)}, bf16[2,512,512]{2,1,0:T(8,128)(2,1)S(1)}, u32[]{:S(2)}, u32[]{:S(2)}) %collective-permute-start.24) | collective-permute-done | bytes 1048608 | tf_op jit(solution)/shard_map/ppermute | solution.py:233
  504.5 11.0 %collective-permute-done.21 = bf16[2,512,512]{2,1,0:T(8,128)(2,1)S(1)} collective-permute-done((bf16[2,512,512]{2,1,0:T(8,128)(2,1)S(1)}, bf16[2,512,512]{2,1,0:T(8,128)(2,1)S(1)}, u32[]{:S(2)}, u32[]{:S(2)}) %collective-permute-start.21) | collective-permute-done | bytes 1048608 | tf_op jit(solution)/shard_map/ppermute | solution.py:233
  524.2 6.2 %collective-permute-done.31.came_ref = bf16[2,256,512]{2,1,0:T(8,128)(2,1)S(1)} collective-permute-done((bf16[2,256,512]{2,1,0:T(8,128)(2,1)S(1)}, bf16[2,256,512]{2,1,0:T(8,128)(2,1)S(1)}, u32[]{:S(2)}, u32[]{:S(2)}) %collective-permute-start.31) | collective-permute-done | bytes 524320 | tf_op jit(solution)/shard_map/ppermute | solution.py:227
  531.4 10.2 %collective-permute-done.28.came_ref = bf16[2,256,512]{2,1,0:T(8,128)(2,1)S(1)} collective-permute-done((bf16[2,256,512]{2,1,0:T(8,128)(2,1)S(1)}, bf16[2,256,512]{2,1,0:T(8,128)(2,1)S(1)}, u32[]{:S(2)}, u32[]{:S(2)}) %collective-permute-start.28) | collective-permute-done | bytes 524320 | tf_op jit(solution)/shard_map/ppermute | solution.py:227
  542.6 9.3 %collective-permute-done.25.came_ref = bf16[2,256,512]{2,1,0:T(8,128)(2,1)S(1)} collective-permute-done((bf16[2,256,512]{2,1,0:T(8,128)(2,1)S(1)}, bf16[2,256,512]{2,1,0:T(8,128)(2,1)S(1)}, u32[]{:S(2)}, u32[]{:S(2)}) %collective-permute-start.25) | collective-permute-done | bytes 524320 | tf_op jit(solution)/shard_map/ppermute | solution.py:227
  553.0 4.6 collective-permute-done.22.came_ref
  (112 shorter events, 103.3 us)
Async XLA Ops:
  10.3 112.2 %collective-permute-start.15 = (bf16[2,256,1024]{2,1,0:T(8,128)(2,1)S(1)}, bf16[2,256,1024]{2,1,0:T(8,128)(2,1)S(1)}, u32[]{:S(2)}, u32[]{:S(2)}) collective-permute-start(bf16[2,256,1024]{2,1,0:T(8,128)(2,1)S(1)} %copies.36), channel_id=1, source_target_pairs={{0,1},{1,0},{2,3},{3,2},{4,5},{5,4},{6,7},{7,6},{8,9},{9,8},{10,11... | collective-permute-start | bytes 3145736 | tf_op jit(solution)/shard_map/ppermute | solution.py:227
  12.0 113.9 %collective-permute-start.10 = (bf16[2,256,1024]{2,1,0:T(8,128)(2,1)S(1)}, bf16[2,256,1024]{2,1,0:T(8,128)(2,1)S(1)}, u32[]{:S(2)}, u32[]{:S(2)}) collective-permute-start(bf16[2,256,1024]{2,1,0:T(8,128)(2,1)S(1)} %copies.32), channel_id=1, source_target_pairs={{0,1},{1,0},{2,3},{3,2},{4,5},{5,4},{6,7},{7,6},{8,9},{9,8},{10,11... | collective-permute-start | bytes 3145736 | tf_op jit(solution)/shard_map/ppermute | solution.py:227
  19.5 109.9 %collective-permute-start.5 = (bf16[2,256,1024]{2,1,0:T(8,128)(2,1)S(1)}, bf16[2,256,1024]{2,1,0:T(8,128)(2,1)S(1)}, u32[]{:S(2)}, u32[]{:S(2)}) collective-permute-start(bf16[2,256,1024]{2,1,0:T(8,128)(2,1)S(1)} %copies.28), channel_id=1, source_target_pairs={{0,1},{1,0},{2,3},{3,2},{4,5},{5,4},{6,7},{7,6},{8,9},{9,8},{10,11... | collective-permute-start | bytes 3145736 | tf_op jit(solution)/shard_map/ppermute | solution.py:227
  30.1 101.3 %collective-permute-start.17 = (bf16[2,512,512]{2,1,0:T(8,128)(2,1)}, bf16[2,512,512]{2,1,0:T(8,128)(2,1)}, u32[]{:S(2)}, u32[]{:S(2)}) collective-permute-start(bf16[2,512,512]{2,1,0:T(8,128)(2,1)} %copies.39.kv0), channel_id=1, source_target_pairs={{0,2},{1,3},{2,4},{3,5},{4,6},{5,7},{6,8},{7,9},{8,10},{9,11},{10,... | collective-permute-start | bytes 3145736 | tf_op jit(solution)/shard_map/ppermute | solution.py:233
  41.3 77.5 %collective-permute-start.1 = (bf16[2,256,512]{2,1,0:T(8,128)(2,1)}, bf16[2,256,512]{2,1,0:T(8,128)(2,1)}, u32[]{:S(2)}, u32[]{:S(2)}) collective-permute-start(bf16[2,256,512]{2,1,0:T(8,128)(2,1)} %copies.26), channel_id=1, source_target_pairs={{0,1},{1,0},{2,3},{3,2},{4,5},{5,4},{6,7},{7,6},{8,9},{9,8},{10,11... | collective-permute-start | bytes 1572872 | tf_op jit(solution)/shard_map/ppermute | solution.py:227
  126.0 47.3 %collective-permute-start.7 = (bf16[2,512,512]{2,1,0:T(8,128)(2,1)}, bf16[2,512,512]{2,1,0:T(8,128)(2,1)}, u32[]{:S(2)}, u32[]{:S(2)}) collective-permute-start(bf16[2,512,512]{2,1,0:T(8,128)(2,1)} %copies.31.kv0), channel_id=1, source_target_pairs={{0,2},{1,3},{2,4},{3,5},{4,6},{5,7},{6,8},{7,9},{8,10},{9,11},{10,... | collective-permute-start | bytes 3145736 | tf_op jit(solution)/shard_map/ppermute | solution.py:233
  129.5 66.2 %collective-permute-start.2 = (bf16[2,512,512]{2,1,0:T(8,128)(2,1)}, bf16[2,512,512]{2,1,0:T(8,128)(2,1)}, u32[]{:S(2)}, u32[]{:S(2)}) collective-permute-start(bf16[2,512,512]{2,1,0:T(8,128)(2,1)} %copies.27.kv0), channel_id=1, source_target_pairs={{0,2},{1,3},{2,4},{3,5},{4,6},{5,7},{6,8},{7,9},{8,10},{9,11},{10,... | collective-permute-start | bytes 3145736 | tf_op jit(solution)/shard_map/ppermute | solution.py:233
  131.4 86.8 %collective-permute-start.18 = (bf16[2,512,512]{2,1,0:T(8,128)(2,1)}, bf16[2,512,512]{2,1,0:T(8,128)(2,1)}, u32[]{:S(2)}, u32[]{:S(2)}) collective-permute-start(bf16[2,512,512]{2,1,0:T(8,128)(2,1)} %collective-permute-done.17.kv1), channel_id=1, source_target_pairs={{0,2},{1,3},{2,4},{3,5},{4,6},{5,7},{6,8},{7,9},{8,10},{9,11},{10,... | collective-permute-start | bytes 3145736 | tf_op jit(solution)/shard_map/ppermute | solution.py:233
  150.8 95.9 %collective-permute-start.13 = (bf16[2,512,512]{2,1,0:T(8,128)(2,1)}, bf16[2,512,512]{2,1,0:T(8,128)(2,1)S(1)}, u32[]{:S(2)}, u32[]{:S(2)}) collective-permute-start(bf16[2,512,512]{2,1,0:T(8,128)(2,1)} %collective-permute-done.12.kv1), channel_id=1, source_target_pairs={{0,2},{1,3},{2,4},{3,5},{4,6},{5,7},{6,8},{7,9},{8,10},{9,11},{10,... | collective-permute-start | bytes 3145736 | tf_op jit(solution)/shard_map/ppermute | solution.py:233
  173.2 100.4 %collective-permute-start.8 = (bf16[2,512,512]{2,1,0:T(8,128)(2,1)}, bf16[2,512,512]{2,1,0:T(8,128)(2,1)S(1)}, u32[]{:S(2)}, u32[]{:S(2)}) collective-permute-start(bf16[2,512,512]{2,1,0:T(8,128)(2,1)} %collective-permute-done.7.kv1), channel_id=1, source_target_pairs={{0,2},{1,3},{2,4},{3,5},{4,6},{5,7},{6,8},{7,9},{8,10},{9,11},{10,... | collective-permute-start | bytes 3145736 | tf_op jit(solution)/shard_map/ppermute | solution.py:233
  195.7 105.0 %collective-permute-start.3 = (bf16[2,512,512]{2,1,0:T(8,128)(2,1)}, bf16[2,512,512]{2,1,0:T(8,128)(2,1)S(1)}, u32[]{:S(2)}, u32[]{:S(2)}) collective-permute-start(bf16[2,512,512]{2,1,0:T(8,128)(2,1)} %collective-permute-done.2.kv1), channel_id=1, source_target_pairs={{0,2},{1,3},{2,4},{3,5},{4,6},{5,7},{6,8},{7,9},{8,10},{9,11},{10,... | collective-permute-start | bytes 3145736 | tf_op jit(solution)/shard_map/ppermute | solution.py:233
  242.2 86.3 %collective-permute-start.29 = (bf16[2,512,512]{2,1,0:T(8,128)(2,1)}, bf16[2,512,512]{2,1,0:T(8,128)(2,1)}, u32[]{:S(2)}, u32[]{:S(2)}) collective-permute-start(bf16[2,512,512]{2,1,0:T(8,128)(2,1)} %get-tuple-element.42), channel_id=1, source_target_pairs={{2,0},{3,1},{4,2},{5,3},{6,4},{7,5},{8,6},{9,7},{10,8},{11,9},{12,... | collective-permute-start | bytes 3145736 | tf_op jit(solution)/shard_map/ppermute | solution.py:233
  271.7 62.8 %collective-permute-start.26 = (bf16[2,512,512]{2,1,0:T(8,128)(2,1)}, bf16[2,512,512]{2,1,0:T(8,128)(2,1)}, u32[]{:S(2)}, u32[]{:S(2)}) collective-permute-start(bf16[2,512,512]{2,1,0:T(8,128)(2,1)} %get-tuple-element.39), channel_id=1, source_target_pairs={{2,0},{3,1},{4,2},{5,3},{6,4},{7,5},{8,6},{9,7},{10,8},{11,9},{12,... | collective-permute-start | bytes 3145736 | tf_op jit(solution)/shard_map/ppermute | solution.py:233
  298.6 39.0 %collective-permute-start.23 = (bf16[2,512,512]{2,1,0:T(8,128)(2,1)}, bf16[2,512,512]{2,1,0:T(8,128)(2,1)}, u32[]{:S(2)}, u32[]{:S(2)}) collective-permute-start(bf16[2,512,512]{2,1,0:T(8,128)(2,1)} %get-tuple-element.36), channel_id=1, source_target_pairs={{2,0},{3,1},{4,2},{5,3},{6,4},{7,5},{8,6},{9,7},{10,8},{11,9},{12,... | collective-permute-start | bytes 3145736 | tf_op jit(solution)/shard_map/ppermute | solution.py:233
  325.7 111.2 %collective-permute-start.20 = (bf16[2,512,512]{2,1,0:T(8,128)(2,1)}, bf16[2,512,512]{2,1,0:T(8,128)(2,1)S(1)}, u32[]{:S(2)}, u32[]{:S(2)}) collective-permute-start(bf16[2,512,512]{2,1,0:T(8,128)(2,1)} %get-tuple-element.33), channel_id=1, source_target_pairs={{2,0},{3,1},{4,2},{5,3},{6,4},{7,5},{8,6},{9,7},{10,8},{11,9},{12,... | collective-permute-start | bytes 3145736 | tf_op jit(solution)/shard_map/ppermute | solution.py:233
  327.7 188.7 %collective-permute-start.19 = (bf16[1,256,1024]{2,1,0:T(8,128)(2,1)S(1)}, bf16[1,256,1024]{2,1,0:T(8,128)(2,1)S(1)}, u32[]{:S(2)}, u32[]{:S(2)}) collective-permute-start(bf16[1,256,1024]{2,1,0:T(8,128)(2,1)S(1)} %get-tuple-element.59), channel_id=1, source_target_pairs={{0,1},{1,0},{2,3},{3,2},{4,5},{5,4},{6,7},{7,6},{8,9},{9,8},{10,11... | collective-permute-start | bytes 1572872 | tf_op jit(solution)/shard_map/ppermute | solution.py:227
  330.0 128.5 %collective-permute-start.30 = (bf16[2,512,512]{2,1,0:T(8,128)(2,1)S(1)}, bf16[2,512,512]{2,1,0:T(8,128)(2,1)S(1)}, u32[]{:S(2)}, u32[]{:S(2)}) collective-permute-start(bf16[2,512,512]{2,1,0:T(8,128)(2,1)S(1)} %add_convert_fusion.1), channel_id=1, source_target_pairs={{2,0},{3,1},{4,2},{5,3},{6,4},{7,5},{8,6},{9,7},{10,8},{11,9},{12,... | collective-permute-start | bytes 3145736 | tf_op jit(solution)/shard_map/ppermute | solution.py:233
  334.5 183.5 %collective-permute-start.14 = (bf16[1,256,1024]{2,1,0:T(8,128)(2,1)S(1)}, bf16[1,256,1024]{2,1,0:T(8,128)(2,1)S(1)}, u32[]{:S(2)}, u32[]{:S(2)}) collective-permute-start(bf16[1,256,1024]{2,1,0:T(8,128)(2,1)S(1)} %get-tuple-element.61), channel_id=1, source_target_pairs={{0,1},{1,0},{2,3},{3,2},{4,5},{5,4},{6,7},{7,6},{8,9},{9,8},{10,11... | collective-permute-start | bytes 1572872 | tf_op jit(solution)/shard_map/ppermute | solution.py:227
  337.6 143.4 %collective-permute-start.27 = (bf16[2,512,512]{2,1,0:T(8,128)(2,1)S(1)}, bf16[2,512,512]{2,1,0:T(8,128)(2,1)S(1)}, u32[]{:S(2)}, u32[]{:S(2)}) collective-permute-start(bf16[2,512,512]{2,1,0:T(8,128)(2,1)S(1)} %add_convert_fusion.3), channel_id=1, source_target_pairs={{2,0},{3,1},{4,2},{5,3},{6,4},{7,5},{8,6},{9,7},{10,8},{11,9},{12,... | collective-permute-start | bytes 3145736 | tf_op jit(solution)/shard_map/ppermute | solution.py:233
  436.9 66.6 %collective-permute-start.24 = (bf16[2,512,512]{2,1,0:T(8,128)(2,1)S(1)}, bf16[2,512,512]{2,1,0:T(8,128)(2,1)S(1)}, u32[]{:S(2)}, u32[]{:S(2)}) collective-permute-start(bf16[2,512,512]{2,1,0:T(8,128)(2,1)S(1)} %add_convert_fusion.5), channel_id=1, source_target_pairs={{2,0},{3,1},{4,2},{5,3},{6,4},{7,5},{8,6},{9,7},{10,8},{11,9},{12,... | collective-permute-start | bytes 3145736 | tf_op jit(solution)/shard_map/ppermute | solution.py:233
  458.5 57.0 %collective-permute-start.21 = (bf16[2,512,512]{2,1,0:T(8,128)(2,1)S(1)}, bf16[2,512,512]{2,1,0:T(8,128)(2,1)S(1)}, u32[]{:S(2)}, u32[]{:S(2)}) collective-permute-start(bf16[2,512,512]{2,1,0:T(8,128)(2,1)S(1)} %add_convert_fusion.7), channel_id=1, source_target_pairs={{2,0},{3,1},{4,2},{5,3},{6,4},{7,5},{8,6},{9,7},{10,8},{11,9},{12,... | collective-permute-start | bytes 3145736 | tf_op jit(solution)/shard_map/ppermute | solution.py:233
  481.0 37.6 %collective-permute-start.9 = (bf16[1,256,1024]{2,1,0:T(8,128)(2,1)S(1)}, bf16[1,256,1024]{2,1,0:T(8,128)(2,1)S(1)}, u32[]{:S(2)}, u32[]{:S(2)}) collective-permute-start(bf16[1,256,1024]{2,1,0:T(8,128)(2,1)S(1)} %get-tuple-element.63), channel_id=1, source_target_pairs={{0,1},{1,0},{2,3},{3,2},{4,5},{5,4},{6,7},{7,6},{8,9},{9,8},{10,11... | collective-permute-start | bytes 1572872 | tf_op jit(solution)/shard_map/ppermute | solution.py:227
  517.9 34.0 %collective-permute-start.25 = (bf16[2,256,512]{2,1,0:T(8,128)(2,1)S(1)}, bf16[2,256,512]{2,1,0:T(8,128)(2,1)S(1)}, u32[]{:S(2)}, u32[]{:S(2)}) collective-permute-start(bf16[2,256,512]{2,1,0:T(8,128)(2,1)S(1)} %get-tuple-element.55), channel_id=1, source_target_pairs={{0,1},{1,0},{2,3},{3,2},{4,5},{5,4},{6,7},{7,6},{8,9},{9,8},{10,11... | collective-permute-start | bytes 1572872 | tf_op jit(solution)/shard_map/ppermute | solution.py:227
  518.6 39.0 %collective-permute-start.22 = (bf16[2,256,512]{2,1,0:T(8,128)(2,1)S(1)}, bf16[2,256,512]{2,1,0:T(8,128)(2,1)S(1)}, u32[]{:S(2)}, u32[]{:S(2)}) collective-permute-start(bf16[2,256,512]{2,1,0:T(8,128)(2,1)S(1)} %get-tuple-element.57), channel_id=1, source_target_pairs={{0,1},{1,0},{2,3},{3,2},{4,5},{5,4},{6,7},{7,6},{8,9},{9,8},{10,11... | collective-permute-start | bytes 1572872 | tf_op jit(solution)/shard_map/ppermute | solution.py:227
  (21 other events, 285.1 us)

commit v2 on v1

v2 whole, which is shorter than its diff:
```python
import functools
import math

import jax
import jax.numpy as jnp
from jax import lax
from jax.experimental import pallas as pl
from jax.experimental.pallas import tpu as pltpu
from jax.sharding import PartitionSpec as P

HEADS = 32
KV_HEADS = 16
HEAD_DIM = 128
WINDOW = 1024
TILE = 128
BLOCK = 512
HALF = 256
HEAD_GROUPS = 2

score_scale = 168.0 ** (-0.5)
exp2_scale = score_scale * math.log2(math.e)

VMEM_LIMIT = 60 * 1024 * 1024
LITTLE = pl.CostEstimate(flops=0, bytes_accessed=1024, transcendentals=0)
ATTENTION = pl.CostEstimate(flops=10000000000, bytes_accessed=1024, transcendentals=0)


def attention_kernel(pieces, starts, part, _, *refs):
    refs = list(refs)

    def take(count):
        taken = refs[:count]
        del refs[:count]
        return taken

    rows = BLOCK // pieces
    q_in = take(2) + take(pieces - 1)
    kv_in = [take(pieces) for _ in range(3)]
    take(1)
    dq_out = take(pieces)
    d_out = take(3)
    q_s, g_s, k_s, v_s, kt_s, dq_s, dk_s, dv_s = refs

    here = part[0]

    def tokens(block, piece):
        place = here if piece == 0 else 1 - here
        return pl.ds(pl.multiple_of(block * BLOCK + place * rows, rows), rows)

    q_s[tokens(0, 0), :] = q_in[0][0]
    g_s[tokens(0, 0), :] = q_in[1][0]
    for i in range(1, pieces):
        q_s[tokens(0, i), :] = q_in[1 + i][0]
        g_s[tokens(0, i), :] = q_in[1 + i][1]
    for block, given in zip((2, 1, 0), kv_in):
        for i in range(pieces):
            k_s[tokens(block, i), :] = given[i][0, 0]
            v_s[tokens(block, i), :] = given[i][0, 1]
    for n in range((WINDOW + BLOCK) // HALF):
        kt_s[n] = k_s[n * HALF : (n + 1) * HALF, :].T
    dk_s[...] = jnp.zeros_like(dk_s)
    dv_s[...] = jnp.zeros_like(dv_s)
    lane = lax.broadcasted_iota(jnp.int32, (1, HALF), 1)
    k_iota = lax.broadcasted_iota(jnp.int32, (HALF, HALF), 0)
    tiles = HALF // TILE
    for j in range(BLOCK // HALF):
        first = jnp.full((1, HALF), starts[tiles * j], jnp.int32)
        for t in range(1, tiles):
            first = jnp.where(lane >= t * TILE, starts[tiles * j + t], first)
        q_pos = WINDOW + j * HALF + lane
        count = WINDOW // HALF + 1
        for head in range(2):
            cols = slice(head * HEAD_DIM, (head + 1) * HEAD_DIM)
            at_q = slice(j * HALF, (j + 1) * HALF)
            q = q_s[at_q, cols]
            g = g_s[at_q, cols]
            scores = []
            top = None
            for i in range(count):
                at = slice((j + i) * HALF, (j + i + 1) * HALF)
                s = lax.dot_general(
                    k_s[at, :], q, (((1,), (1,)), ((), ())), preferred_element_type=jnp.float32
                )
                k_pos = (j + i) * HALF + k_iota
                visible = k_pos >= first
                if i == 0:
                    visible = visible & (k_pos > q_pos - WINDOW)
                if i == count - 1:
                    visible = visible & (k_pos <= q_pos)
                s = jnp.where(visible, s, -jnp.inf)
                peak = jnp.max(s, axis=0, keepdims=True)
                top = peak if top is None else jnp.maximum(top, peak)
                scores.append(s)
            shift = top * exp2_scale
            weights, grads = [], []
            total, inner = None, None
            for i in range(count):
                at = slice((j + i) * HALF, (j + i + 1) * HALF)
                w = jnp.exp2(scores[i] * exp2_scale - shift)
                dp = lax.dot_general(
                    v_s[at, :], g, (((1,), (1,)), ((), ())), preferred_element_type=jnp.float32
                )
                part_sum = jnp.sum(w, axis=0, keepdims=True)
                mixed = jnp.sum(w * dp, axis=0, keepdims=True)
                total = part_sum if total is None else total + part_sum
                inner = mixed if inner is None else inner + mixed
                weights.append(w)
                grads.append(dp)
            inverse = 1.0 / total
            delta = inner * inverse
            dq_t = None
            for i in range(count):
                at = slice((j + i) * HALF, (j + i + 1) * HALF)
                probs = weights[i] * inverse
                ds = (probs * (grads[i] - delta)).astype(jnp.bfloat16)
                low = probs.astype(jnp.bfloat16)
                dv_s[at, :] += jnp.dot(low, g, preferred_element_type=jnp.float32)
                dk_s[at, :] += jnp.dot(ds, q, preferred_element_type=jnp.float32)
                term = jnp.dot(kt_s[j + i], ds, preferred_element_type=jnp.float32)
                dq_t = term if dq_t is None else dq_t + term
            dq_s[at_q, cols] = (dq_t.T * score_scale).astype(jnp.bfloat16)
    for i in range(pieces):
        dq_out[i][0] = dq_s[tokens(0, i), :]
        for block, out in zip((2, 1, 0), d_out):
            out[i, 0] = (dk_s[tokens(block, i), :] * score_scale).astype(jnp.bfloat16)
            out[i, 1] = dv_s[tokens(block, i), :].astype(jnp.bfloat16)


def attention(token, starts, part, q_own, q_came, blocks, cols):
    pieces = len(blocks[0])
    rows = BLOCK // pieces
    heads = cols // HEAD_DIM
    wide = 2 * HEAD_DIM
    keys = WINDOW + BLOCK
    bf16 = jnp.bfloat16

    def piece(lead, width):
        return pl.BlockSpec((*lead, rows, width), lambda h, *_: (0,) * (len(lead) + 1) + (h,))

    moved = piece((pieces, 2), HEAD_DIM)
    flat = [given for block in blocks for given in block]
    operands = [a for a, _ in q_own] + q_came + [a for a, _ in flat]
    in_specs = [pl.BlockSpec((1, rows, wide), index) for _, index in q_own]
    in_specs += [piece((2,), wide)] * len(q_came)
    in_specs += [
        pl.BlockSpec((1, 2, rows, HEAD_DIM), lambda h, *_, at=at: (at, 0, 0, h)) for _, at in flat
    ]
    anywhere = pl.BlockSpec(memory_space=pl.ANY)
    return pl.pallas_call(
        functools.partial(attention_kernel, pieces),
        grid_spec=pltpu.PrefetchScalarGridSpec(
            num_scalar_prefetch=2,
            grid=(heads,),
            in_specs=[anywhere] + in_specs,
            out_specs=[anywhere] + [piece((1,), wide)] * pieces + [moved] * 3,
            scratch_shapes=[
                pltpu.VMEM((BLOCK, wide), bf16),
                pltpu.VMEM((BLOCK, wide), bf16),
                pltpu.VMEM((keys, HEAD_DIM), bf16),
                pltpu.VMEM((keys, HEAD_DIM), bf16),
                pltpu.VMEM((keys // HALF, HEAD_DIM, HALF), bf16),
                pltpu.VMEM((BLOCK, wide), bf16),
                pltpu.VMEM((keys, HEAD_DIM), jnp.float32),
                pltpu.VMEM((keys, HEAD_DIM), jnp.float32),
            ],
        ),
        out_shape=[jax.ShapeDtypeStruct(token.shape, token.dtype)]
        + [jax.ShapeDtypeStruct((1, rows, 2 * cols), bf16)] * pieces
        + [jax.ShapeDtypeStruct((pieces, 2, rows, cols), bf16)] * 3,
        input_output_aliases={2: 0},
        compiler_params=pltpu.CompilerParams(vmem_limit_bytes=VMEM_LIMIT),
        cost_estimate=ATTENTION,
        name="attention",
    )(starts, part, token, *operands)


def call_copies(kernel, token, part, operands, in_specs, out_specs, out_shape, grid=(1,), aliases=None):
    ins, outs = len(operands), len(out_shape)

    def body(part_ref, _, *refs):
        kernel(part_ref, *refs[:ins], *refs[ins + 1 :])

    anywhere = pl.BlockSpec(memory_space=pl.ANY)
    results = pl.pallas_call(
        body,
        grid_spec=pltpu.PrefetchScalarGridSpec(
            num_scalar_prefetch=1,
            grid=grid,
            in_specs=[anywhere] + in_specs,
            out_specs=[anywhere] + out_specs,
        ),
        out_shape=[jax.ShapeDtypeStruct(token.shape, token.dtype)] + out_shape,
        input_output_aliases={1: 0, **{i + 1: o + 1 for i, o in (aliases or {}).items()}},
        compiler_params=pltpu.CompilerParams(vmem_limit_bytes=VMEM_LIMIT),
        cost_estimate=LITTLE,
        name="copies",
    )(part, token, *operands)
    return results[0], results[1:]


def pack(token, part, arrays, seq, group, groups, both):
    rows, width = arrays[0].shape[1], arrays[0].shape[2]
    cols = width // (2 * groups)
    count = len(arrays)
    results = 2 if both else 1

    def kernel(_, *refs):
        for n in range(count * results):
            refs[count * results + n // count][n % count] = refs[n][0]

    theirs = pl.BlockSpec((1, rows, cols), lambda _, y: (seq, 0, (1 - y[0]) * groups + group))
    ours = pl.BlockSpec((1, rows, cols), lambda _, y: (seq, 0, y[0] * groups + group))
    shape = (count, rows, cols)
    return call_copies(
        kernel,
        token,
        part,
        list(arrays) * results,
        [theirs] * count + [ours] * (count * (results - 1)),
        [pl.BlockSpec(shape, lambda *_: (0, 0, 0))] * results,
        [jax.ShapeDtypeStruct(shape, jnp.bfloat16)] * results,
    )


def assemble(token, part, arrays, came, seq, group, groups):
    rows, width = arrays[0].shape[1], arrays[0].shape[2]
    cols = width // (2 * groups)
    count = len(arrays)

    def kernel(_, *refs):
        out = refs[count + 1]
        for n in range(count):
            out[0, n] = refs[n][0]
            out[1, n] = refs[count][n]

    ours = pl.BlockSpec((1, rows, cols), lambda _, y: (seq, 0, y[0] * groups + group))
    shape = (2, count, rows, cols)
    token, results = call_copies(
        kernel,
        token,
        part,
        list(arrays) + [came],
        [ours] * count + [pl.BlockSpec(came.shape, lambda *_: (0, 0, 0))],
        [pl.BlockSpec(shape, lambda *_: (0, 0, 0, 0))],
        [jax.ShapeDtypeStruct(shape, jnp.bfloat16)],
    )
    return token, results[0]


def sums(token, part, one, other, apart):
    pieces, count, rows, cols = one.shape

    def kernel(_, one_ref, other_ref, *outs):
        for i in range(pieces):
            value = added(one_ref[i], other_ref[i])
            if apart:
                outs[i][...] = value
            else:
                outs[0][i] = value

    block = pl.BlockSpec((pieces, 1, rows, cols), lambda n, _: (0, n, 0, 0))
    shapes = [one.shape]
    out_specs = [block]
    if apart:
        shapes = [one.shape[1:]] * pieces
        out_specs = [pl.BlockSpec((1, rows, cols), lambda n, _: (n, 0, 0))] * pieces
    token, results = call_copies(
        kernel,
        token,
        part,
        [one, other],
        [block, block],
        out_specs,
        [jax.ShapeDtypeStruct(shape, jnp.bfloat16) for shape in shapes],
        grid=(count,),
    )
    return token, results if apart else results[0]


def joined(token, part, arrays):
    count, rows, cols = arrays[0].shape
    pieces = len(arrays)

    def kernel(_, *refs):
        for i in range(pieces):
            refs[pieces][i] = refs[i][...]

    token, results = call_copies(
        kernel,
        token,
        part,
        arrays,
        [pl.BlockSpec((1, rows, cols), lambda n, _: (n, 0, 0))] * pieces,
        [pl.BlockSpec((pieces, 1, rows, cols), lambda n, _: (0, n, 0, 0))],
        [jax.ShapeDtypeStruct((pieces, count, rows, cols), jnp.bfloat16)],
        grid=(count,),
    )
    return token, results[0]


def place(token, part, ours, theirs, outs, shape, seq, group, groups):
    count, rows, cols = ours[0].shape
    terms = len(ours)
    old = [] if outs is None else list(outs)

    def kernel(_, *refs):
        results = refs[2 * terms + len(old) :]
        for step in range(2):

            @pl.when(pl.program_id(0) == step)
            def _():
                given = refs[step * terms : (step + 1) * terms]
                for n in range(count):
                    value = given[0][n]
                    if terms == 2:
                        value = added(value, given[1][n])
                    results[n][0] = value

    whole = pl.BlockSpec((count, rows, cols), lambda *_: (0, 0, 0))
    block = pl.BlockSpec(
        (1, rows, cols), lambda i, y: (seq, 0, (y[0] + i - 2 * i * y[0]) * groups + group)
    )
    return call_copies(
        kernel,
        token,
        part,
        list(ours) + list(theirs) + old,
        [whole] * (2 * terms) + [pl.BlockSpec(memory_space=pl.ANY)] * len(old),
        [block] * count,
        [jax.ShapeDtypeStruct(shape, jnp.bfloat16)] * count,
        grid=(2,),
        aliases={2 * terms + 1 + n: n for n in range(len(old))},
    )


def swapped(value):
    pairs = [(i, i ^ 1) for i in range(lax.axis_size("fsdp"))]
    return lax.ppermute(value, "fsdp", pairs)


def shifted(value, by, across=0):
    count = lax.axis_size("ctx") * lax.axis_size("fsdp")
    pairs = [(i, (i + by) ^ across) for i in range(count) if 0 <= i + by < count]
    return lax.ppermute(value, ("ctx", "fsdp"), pairs)


def regrouped(value, split_axis, concat_axis, split):
    groups = lax.axis_size("fsdp")
    members = [list(range(n, n + split)) for n in range(0, groups, split)]
    return lax.all_to_all(
        value, "fsdp", split_axis, concat_axis, axis_index_groups=members, tiled=True
    )


def to_heads(arrays, seq, group, groups, split):
    rows, width = arrays[0].shape[1], arrays[0].shape[2]
    cols = width // split // groups
    send = jnp.stack([a[seq].reshape(rows, split, groups, cols)[:, :, group] for a in arrays])
    return regrouped(send, 2, 1, split).reshape(len(arrays), split * rows, cols)


def to_tokens(value, outs, shape, seq, group, groups, split):
    count, length, cols = value.shape
    rows = length // split
    whole = regrouped(value.reshape(count, split, rows, cols), 1, 1, split)
    results = []
    for n in range(count):
        result = jnp.zeros(shape, jnp.bfloat16) if outs is None else outs[n]
        for p in range(split):
            left = (p * groups + group) * cols
            result = lax.dynamic_update_slice(result, whole[n, p][None], (seq, 0, left))
        results.append(result)
    return results


def tie(one, other):
    return lax.optimization_barrier((one, other))


def added(one, other):
    return (one.astype(jnp.float32) + other.astype(jnp.float32)).astype(jnp.bfloat16)


def body(query, key, value, grad_out, tile_start):
    seqs, rows, _ = query.shape
    split = BLOCK // rows
    position = lax.axis_index("fsdp")
    blocks = lax.axis_size("fsdp") // split
    block = lax.axis_index("ctx") * blocks + position // split
    per_block = BLOCK // TILE
    tiles = lax.dynamic_slice_in_dim(tile_start, block * per_block, per_block, 1)
    starts = tiles * TILE - (block * BLOCK - WINDOW)
    paired = split == 2
    part = jnp.full((1,), position % 2 if paired else 0, jnp.int32)
    groups = min(HEAD_GROUPS, KV_HEADS // split)
    cols = KV_HEADS * HEAD_DIM // split // groups
    heads = cols // HEAD_DIM
    pieces = 2 if paired else 1
    chunks = [(s, h, groups) for s in range(seqs) for h in range(groups)]
    count = len(chunks)
    kv_arrays, qg_arrays = (key, value), (query, grad_out)
    straight = [paired and c == count - 1 for c in range(count)]
    kv_send, kv_came, qg_came, q_own, kv0, kv1, kv2 = ([None] * count for _ in range(7))
    dq, dq_came, d0, d1, d2, d0_came = ([None] * count for _ in range(6))
    d1_came, back, d0_more, total, total_came = ([None] * count for _ in range(5))
    outs_q, outs_kv = None, None
    token = jnp.zeros((8, 128), jnp.float32)

    def pack_kv(c):
        nonlocal token
        if not paired:
            kv0[c] = to_heads(kv_arrays, *chunks[c], split)[None]
            return
        token, results = pack(token, part, kv_arrays, *chunks[c], c == 0)
        kv_send[c] = results[0]
        if c == 0:
            kv0[c] = (results[1], results[0])

    def swap_kv(c):
        nonlocal token
        if paired:
            kv_send[c], token = tie(kv_send[c], token)
            with jax.named_scope(f"kv_swap_{c}"):
                kv_came[c] = swapped(kv_send[c])

    def wait_kv(c):
        nonlocal token
        if paired:
            kv_came[c], token = tie(kv_came[c], token)

    def swap_qg(c):
        nonlocal token
        if not paired:
            qg = to_heads(qg_arrays, *chunks[c], split)
            q_own[c] = [(qg, lambda h, *_, n=n: (n, 0, h)) for n in range(2)]
            return
        seq, group, _ = chunks[c]

        def own(h, _, y):
            return (seq, 0, (y[0] * groups + group) * heads + h)

        q_own[c] = [(a, own) for a in qg_arrays]
        token, results = pack(token, part, qg_arrays, *chunks[c], False)
        with jax.named_scope(f"qg_swap_{c}"):
            qg_came[c] = swapped(results[0])

    def wait_qg(c):
        nonlocal token
        if paired:
            qg_came[c], token = tie(qg_came[c], token)

    def hop_1(c):
        nonlocal token
        if paired and c > 0:
            token, kv0[c] = assemble(token, part, kv_arrays, kv_came[c], *chunks[c])
        with jax.named_scope(f"kv_hop_1_{c}"):
            if paired and c == 0:
                kv1[c] = [shifted(a, split, across) for across, a in enumerate(kv0[c])]
            else:
                kv1[c] = shifted(kv0[c], split)

    def hop_2(c):
        nonlocal token
        if paired and c == 0:
            token, kv1[c] = joined(token, part, kv1[c])
        else:
            kv1[c], token = tie(kv1[c], token)
        with jax.named_scope(f"kv_hop_2_{c}"):
            kv2[c] = shifted(kv1[c], split)

    def attend(c):
        nonlocal token
        if paired and c == 0:
            blocks = [[(kv0[c][0][None], 0), (kv_came[c][None], 0)]]
        else:
            blocks = [[(kv0[c], i) for i in range(pieces)]]
        blocks += [[(a, i) for i in range(pieces)] for a in (kv1[c], kv2[c])]
        came = [qg_came[c]] if paired else []
        token, *results = attention(
            token, starts[chunks[c][0]], part, q_own[c], came, blocks, cols
        )
        dq[c] = results[:-3]
        d0[c], d1[c], d2[c] = results[-3:]

    def wait_hop(c):
        nonlocal token
        kv2[c], token = tie(kv2[c], token)

    def return_1(c):
        nonlocal token
        d2[c], token = tie(d2[c], token)
        with jax.named_scope(f"back_1_{c}"):
            d1_came[c] = shifted(d2[c], -split)

    def return_2(c):
        nonlocal token
        apart = straight[c]
        token, back[c] = sums(token, part, d1[c], d1_came[c], apart)
        with jax.named_scope(f"back_2_{c}"):
            if apart:
                d0_more[c] = [shifted(a, -split, across) for across, a in enumerate(back[c])]
            else:
                d0_more[c] = shifted(back[c], -split)

    def swap_grad_kv(c):
        nonlocal token
        if straight[c]:
            send, token = tie(d0[c][1], token)
            with jax.named_scope(f"grad_kv_swap_{c}"):
                d0_came[c] = swapped(send)
        elif paired:
            token, total[c] = sums(token, part, d0[c], d0_more[c], True)
            with jax.named_scope(f"grad_kv_swap_{c}"):
                total_came[c] = swapped(total[c][1])

    def wait_grad_kv(c):
        nonlocal token
        if straight[c]:
            d0_came[c], token = tie(d0_came[c], token)

    def swap_grad_q(c):
        nonlocal token
        if paired:
            dq[c][1], token = tie(dq[c][1], token)
            with jax.named_scope(f"grad_q_swap_{c}"):
                dq_came[c] = swapped(dq[c][1])

    def put_q(c):
        nonlocal token, outs_q
        if paired:
            token, outs_q = place(
                token, part, dq[c][:1], [dq_came[c]], outs_q, query.shape, *chunks[c]
            )
        else:
            outs_q = to_tokens(dq[c][0], outs_q, query.shape, *chunks[c], split)

    def put_kv(c):
        nonlocal token, outs_kv
        if not paired:
            token, total[c] = sums(token, part, d0[c], d0_more[c], True)
            outs_kv = to_tokens(total[c][0], outs_kv, key.shape, *chunks[c], split)
            return
        if straight[c]:
            ours, theirs = [d0[c][0], d0_more[c][0]], [d0_came[c], d0_more[c][1]]
        else:
            ours, theirs = total[c][:1], [total_came[c]]
        token, outs_kv = place(token, part, ours, theirs, outs_kv, key.shape, *chunks[c])

    stages = [pack_kv, swap_kv, swap_qg, hop_1, hop_2, attend, return_1, return_2]
    stages += [swap_grad_kv, swap_grad_q, put_q, put_kv]
    plan = [(stage, c) for c in range(count) for stage in stages]
    if count == 4:
        plan = [
            (pack_kv, 0), (hop_1, 0), (pack_kv, 1), (swap_kv, 1), (pack_kv, 2), (pack_kv, 3),
            (hop_1, 1), (swap_kv, 2), (swap_kv, 0), (hop_2, 0), (hop_1, 2), (swap_qg, 0),
            (wait_kv, 0), (swap_kv, 3), (hop_2, 1), (hop_1, 3), (wait_qg, 0), (swap_qg, 1),
            (hop_2, 2), (attend, 0), (hop_2, 3), (wait_qg, 1), (swap_qg, 2), (attend, 1),
            (return_1, 0), (wait_qg, 2), (swap_qg, 3), (attend, 2), (wait_hop, 3), (return_1, 1),
            (wait_qg, 3), (return_2, 0), (swap_grad_q, 0), (attend, 3), (return_1, 2), (put_q, 0),
            (swap_grad_q, 1), (return_2, 1), (return_1, 3), (swap_grad_kv, 0), (put_q, 1),
            (swap_grad_q, 2), (return_2, 2), (put_kv, 0), (put_q, 2), (swap_grad_kv, 3),
            (swap_grad_q, 3), (swap_grad_kv, 1), (put_q, 3), (wait_grad_kv, 3), (return_2, 3),
            (put_kv, 1), (swap_grad_kv, 2), (put_kv, 3), (put_kv, 2),
        ]
    for stage, c in plan:
        stage(c)
    return outs_q[0], outs_kv[0], outs_kv[1]


def solution(mesh):
    tokens = P(None, ("ctx", "fsdp"), None)
    return jax.shard_map(
        body,
        mesh=mesh,
        in_specs=(tokens, tokens, tokens, tokens, P()),
        out_specs=(tokens, tokens, tokens),
        check_vma=False,
    )
```

time: 560 us -> 392 us (0.70)
  waiting for transfers between devices: 336 us -> 121 us
  Pallas kernels: 125 us -> 159 us
  local copies, waits for them, and re-layouts: 13.8 us -> 21 us
  starting transfers between devices: 75.8 us -> 82.1 us
  other arithmetic: 6.22 us -> 0.07 us
    ppermute x16 -> x18, waiting for transfers between devices: 217 us -> 70.5 us  [shifted(): return lax.ppermute(value, ('ctx', 'fsdp'), pairs)]
    ppermute x16, waiting for transfers between devices: 120 us -> 51 us  [swapped(): return lax.ppermute(value, 'fsdp', pairs)]
    pallas_call x28 -> x31, Pallas kernels: 125 us -> 159 us  [the longest x4 98.2 us: attention(): pl.pallas_call(functools.partial(attention_kernel, pieces), grid_spec=plt...]
    ppermute x16 -> x18, starting transfers between devices: 57.9 us -> 66 us  [shifted(): return lax.ppermute(value, ('ctx', 'fsdp'), pairs)]
    convert_element_type x8 -> x0, other arithmetic: 6.14 us -> none  [added(): (one.astype(jnp.float32) + other.astype(jnp.float32)).astype(jnp.bfloat16)]
    unnamed x26 -> x54, local copies, waits for them, and re-layouts: 13.2 us -> 17.6 us
  transfers between devices with their start and end apart: 32 -> 34, of which waited for: 18 -> 12; matrix products, arithmetic and copies ran while one was open for 1% -> 1% of each run, Pallas kernels for 22% -> 40%
where the time goes in v2:
time: 392 us; the launch traced here: 385 us
  Pallas kernels  159 us (41%)
  waiting for transfers between devices  121 us (31%)
  starting transfers between devices  82.1 us (21%)
  local copies, waits for them, and re-layouts  21 us (5%)
    pallas_call x4, Pallas kernels, attention(): pl.pallas_call(functools.partial(attention_kernel, pieces), grid_spec=plt...  98.2 us
    ppermute x18, waiting for transfers between devices, shifted(): return lax.ppermute(value, ('ctx', 'fsdp'), pairs)  70.5 us
    ppermute x18, starting transfers between devices, shifted(): return lax.ppermute(value, ('ctx', 'fsdp'), pairs)  66 us
    pallas_call x27, Pallas kernels, call_copies(): pl.pallas_call(body, grid_spec=pltpu.PrefetchScalarGridSpec(num_scalar_pr...  61.2 us
    ppermute x16, waiting for transfers between devices, swapped(): return lax.ppermute(value, 'fsdp', pairs)  51 us
    unnamed x54, local copies, waits for them, and re-layouts  17.6 us
    ppermute x16, starting transfers between devices, swapped(): return lax.ppermute(value, 'fsdp', pairs)  16.1 us
  transfers between devices with their start and end apart: 34, of which 12 were waited for; matrix products, arithmetic and copies ran while one was open for 1% of the time, Pallas kernels for 40%

profile of v2, /device:TPU:10, one launch (start us, length us, event | category | flops | bytes accessed | tf_op | source)
XLA Modules:
  0.0 385.1 jit_solution(2792647356094645823)
XLA Ops:
  10.3 3.5 collective-permute-start.1
  17.5 12.9 %collective-permute-done.refs_2_ = bf16[2,256,512]{2,1,0:T(8,128)(2,1)S(1)} collective-permute-done((bf16[2,256,512]{2,1,0:T(8,128)(2,1)}, bf16[2,256,512]{2,1,0:T(8,128)(2,1)S(1)}, u32[]{:S(2)}, u32[]{:S(2)}) %collective-permute-start) | collective-permute-done | bytes 524320 | tf_op jit(solution)/shard_map/kv_swap_1/ppermute | solution.py:338
  42.7 5.9 %collective-permute-done.3.refs_2_ = bf16[2,256,512]{2,1,0:T(8,128)(2,1)S(1)} collective-permute-done((bf16[2,256,512]{2,1,0:T(8,128)(2,1)}, bf16[2,256,512]{2,1,0:T(8,128)(2,1)S(1)}, u32[]{:S(2)}, u32[]{:S(2)}) %collective-permute-start.3) | collective-permute-done | bytes 524320 | tf_op jit(solution)/shard_map/kv_swap_2/ppermute | solution.py:338
  55.8 3.5 collective-permute-start.4
  59.2 3.5 collective-permute-start.9
  64.0 27.5 %collective-permute-done.8.refs_2_ = bf16[2,256,512]{2,1,0:T(8,128)(2,1)S(1)} collective-permute-done((bf16[2,256,512]{2,1,0:T(8,128)(2,1)}, bf16[2,256,512]{2,1,0:T(8,128)(2,1)S(1)}, u32[]{:S(2)}, u32[]{:S(2)}) %collective-permute-start.8) | collective-permute-done | bytes 524320 | tf_op jit(solution)/shard_map/kv_swap_3/ppermute | solution.py:338
  108.8 24.6 %attention.4 = (f32[8,128]{1,0:T(8,128)}, bf16[1,256,1024]{2,1,0:T(8,128)(2,1)}, bf16[1,256,1024]{2,1,0:T(8,128)(2,1)}, bf16[2,2,256,512]{3,2,1,0:T(8,128)(2,1)}...) custom-call(s32[4]{0:T(128)} %get-tuple-element.269.starts, ...), custom_call_target="tpu_custom_call", output_to_operand_aliasing={{0}: (2, {})} | custom-call | flops 10000000000 | bytes 1024 | tf_op jit(solution)/shard_map/attention/pallas_call | solution.py:149
  141.2 3.7 collective-permute-start.15
  144.8 8.9 %collective-permute-done.13.refs_7_.refs_8_ = bf16[2,2,256,512]{3,2,1,0:T(8,128)(2,1)} collective-permute-done((bf16[2,2,256,512]{3,2,1,0:T(8,128)(2,1)S(1)}, bf16[2,2,256,512]{3,2,1,0:T(8,128)(2,1)}, u32[]{:S(2)}, u32[]{:S(2)}) %collective-permute-start.13) | collective-permute-done | bytes 1048608 | tf_op jit(solution)/shard_map/kv_hop_2_1/ppermute | solution.py:344
  153.7 24.6 %attention.5 = (f32[8,128]{1,0:T(8,128)}, bf16[1,256,1024]{2,1,0:T(8,128)(2,1)}, bf16[1,256,1024]{2,1,0:T(8,128)(2,1)}, bf16[2,2,256,512]{3,2,1,0:T(8,128)(2,1)}...) custom-call(s32[4]{0:T(128)} %get-tuple-element.269.starts, ...), custom_call_target="tpu_custom_call", output_to_operand_aliasing={{0}: (2, {})} | custom-call | flops 10000000000 | bytes 1024 | tf_op jit(solution)/shard_map/attention/pallas_call | solution.py:149
  182.2 4.3 %collective-permute-start.17 = (bf16[2,2,256,512]{3,2,1,0:T(8,128)(2,1)}, bf16[2,2,256,512]{3,2,1,0:T(8,128)(2,1)S(1)}, u32[]{:S(2)}, u32[]{:S(2)}) collective-permute-start(bf16[2,2,256,512]{3,2,1,0:T(8,128)(2,1)} %get-tuple-element.193), channel_id=1, source_target_pairs={{2,0},{3,1},{4,2},{5,3},{6,4},{7,5},{8,6},{9,7},{10,8},{11,9},{12,... | collective-permute-start | bytes 3145736 | tf_op jit(solution)/shard_map/back_1_0/ppermute | solution.py:344
  186.6 24.5 %attention.6 = (f32[8,128]{1,0:T(8,128)}, bf16[1,256,1024]{2,1,0:T(8,128)(2,1)}, bf16[1,256,1024]{2,1,0:T(8,128)(2,1)}, bf16[2,2,256,512]{3,2,1,0:T(8,128)(2,1)}...) custom-call(s32[4]{0:T(128)} %get-tuple-element.270.starts, ...), custom_call_target="tpu_custom_call", output_to_operand_aliasing={{0}: (2, {})} | custom-call | flops 10000000000 | bytes 1024 | tf_op jit(solution)/shard_map/attention/pallas_call | solution.py:149
  217.8 7.5 %collective-permute-start.20 = (bf16[2,2,256,512]{3,2,1,0:T(8,128)(2,1)}, bf16[2,2,256,512]{3,2,1,0:T(8,128)(2,1)S(1)}, u32[]{:S(2)}, u32[]{:S(2)}) collective-permute-start(bf16[2,2,256,512]{3,2,1,0:T(8,128)(2,1)} %get-tuple-element.215), channel_id=1, source_target_pairs={{2,0},{3,1},{4,2},{5,3},{6,4},{7,5},{8,6},{9,7},{10,8},{11,9},{12,... | collective-permute-start | bytes 3145736 | tf_op jit(solution)/shard_map/back_2_0/ppermute | solution.py:344
  225.3 24.5 %attention.7 = (f32[8,128]{1,0:T(8,128)}, bf16[1,256,1024]{2,1,0:T(8,128)(2,1)}, bf16[1,256,1024]{2,1,0:T(8,128)(2,1)}, bf16[2,2,256,512]{3,2,1,0:T(8,128)(2,1)}...) custom-call(s32[4]{0:T(128)} %get-tuple-element.270.starts, ...), custom_call_target="tpu_custom_call", output_to_operand_aliasing={{0}: (2, {})} | custom-call | flops 10000000000 | bytes 1024 | tf_op jit(solution)/shard_map/attention/pallas_call | solution.py:149
  249.8 6.5 %collective-permute-start.22 = (bf16[2,2,256,512]{3,2,1,0:T(8,128)(2,1)}, bf16[2,2,256,512]{3,2,1,0:T(8,128)(2,1)S(1)}, u32[]{:S(2)}, u32[]{:S(2)}) collective-permute-start(bf16[2,2,256,512]{3,2,1,0:T(8,128)(2,1)} %get-tuple-element.223), channel_id=1, source_target_pairs={{2,0},{3,1},{4,2},{5,3},{6,4},{7,5},{8,6},{9,7},{10,8},{11,9},{12,... | collective-permute-start | bytes 3145736 | tf_op jit(solution)/shard_map/back_1_2/ppermute | solution.py:344
  263.1 4.0 %collective-permute-start.25 = (bf16[2,2,256,512]{3,2,1,0:T(8,128)(2,1)}, bf16[2,2,256,512]{3,2,1,0:T(8,128)(2,1)S(1)}, u32[]{:S(2)}, u32[]{:S(2)}) collective-permute-start(bf16[2,2,256,512]{3,2,1,0:T(8,128)(2,1)} %get-tuple-element.235), channel_id=1, source_target_pairs={{2,0},{3,1},{4,2},{5,3},{6,4},{7,5},{8,6},{9,7},{10,8},{11,9},{12,... | collective-permute-start | bytes 3145736 | tf_op jit(solution)/shard_map/back_2_1/ppermute | solution.py:344
  277.7 11.1 %collective-permute-done.22.refs_1_ = bf16[2,2,256,512]{3,2,1,0:T(8,128)(2,1)S(1)} collective-permute-done((bf16[2,2,256,512]{3,2,1,0:T(8,128)(2,1)}, bf16[2,2,256,512]{3,2,1,0:T(8,128)(2,1)S(1)}, u32[]{:S(2)}, u32[]{:S(2)}) %collective-permute-start.22) | collective-permute-done | bytes 1048608 | tf_op jit(solution)/shard_map/back_1_2/ppermute | solution.py:344
  303.9 7.5 %collective-permute-done.25.refs_1_ = bf16[2,2,256,512]{3,2,1,0:T(8,128)(2,1)S(1)} collective-permute-done((bf16[2,2,256,512]{3,2,1,0:T(8,128)(2,1)}, bf16[2,2,256,512]{3,2,1,0:T(8,128)(2,1)S(1)}, u32[]{:S(2)}, u32[]{:S(2)}) %collective-permute-start.25) | collective-permute-done | bytes 1048608 | tf_op jit(solution)/shard_map/back_2_1/ppermute | solution.py:344
  317.3 4.6 %collective-permute-done.27.refs_2_ = bf16[2,256,512]{2,1,0:T(8,128)(2,1)S(1)} collective-permute-done((bf16[2,256,512]{2,1,0:T(8,128)(2,1)}, bf16[2,256,512]{2,1,0:T(8,128)(2,1)S(1)}, u32[]{:S(2)}, u32[]{:S(2)}) %collective-permute-start.27) | collective-permute-done | bytes 524320 | tf_op jit(solution)/shard_map/grad_kv_swap_3/ppermute | solution.py:338
  321.9 11.9 %collective-permute-done.28.refs_1_ = bf16[2,2,256,512]{3,2,1,0:T(8,128)(2,1)S(1)} collective-permute-done((bf16[2,2,256,512]{3,2,1,0:T(8,128)(2,1)}, bf16[2,2,256,512]{3,2,1,0:T(8,128)(2,1)S(1)}, u32[]{:S(2)}, u32[]{:S(2)}) %collective-permute-start.28) | collective-permute-done | bytes 1048608 | tf_op jit(solution)/shard_map/back_1_3/ppermute | solution.py:344
  339.1 4.5 %collective-permute-start.32 = (bf16[2,256,512]{2,1,0:T(8,128)(2,1)}, bf16[2,256,512]{2,1,0:T(8,128)(2,1)S(1)}, u32[]{:S(2)}, u32[]{:S(2)}) collective-permute-start(bf16[2,256,512]{2,1,0:T(8,128)(2,1)} %get-tuple-element.257), channel_id=1, source_target_pairs={{2,1},{3,0},{4,3},{5,2},{6,5},{7,4},{8,7},{9,6},{10,9},{11,8},{12,... | collective-permute-start | bytes 1572872 | tf_op jit(solution)/shard_map/back_2_3/ppermute | solution.py:344
  346.6 9.7 %collective-permute-done.30.refs_1_ = bf16[2,2,256,512]{3,2,1,0:T(8,128)(2,1)S(1)} collective-permute-done((bf16[2,2,256,512]{3,2,1,0:T(8,128)(2,1)}, bf16[2,2,256,512]{3,2,1,0:T(8,128)(2,1)S(1)}, u32[]{:S(2)}, u32[]{:S(2)}) %collective-permute-start.30) | collective-permute-done | bytes 1048608 | tf_op jit(solution)/shard_map/back_2_2/ppermute | solution.py:344
  360.0 7.5 %collective-permute-done.31.refs_1_ = bf16[2,256,512]{2,1,0:T(8,128)(2,1)S(1)} collective-permute-done((bf16[2,256,512]{2,1,0:T(8,128)(2,1)}, bf16[2,256,512]{2,1,0:T(8,128)(2,1)S(1)}, u32[]{:S(2)}, u32[]{:S(2)}) %collective-permute-start.31) | collective-permute-done | bytes 524320 | tf_op jit(solution)/shard_map/back_2_3/ppermute | solution.py:344
  367.5 11.1 %collective-permute-done.32.refs_3_ = bf16[2,256,512]{2,1,0:T(8,128)(2,1)S(1)} collective-permute-done((bf16[2,256,512]{2,1,0:T(8,128)(2,1)}, bf16[2,256,512]{2,1,0:T(8,128)(2,1)S(1)}, u32[]{:S(2)}, u32[]{:S(2)}) %collective-permute-start.32) | collective-permute-done | bytes 524320 | tf_op jit(solution)/shard_map/back_2_3/ppermute | solution.py:344
  (133 shorter events, 126.4 us)
Async XLA Ops:
  6.9 32.1 %collective-permute-start.2 = (bf16[2,256,512]{2,1,0:T(8,128)(2,1)}, bf16[2,256,512]{2,1,0:T(8,128)(2,1)S(1)}, u32[]{:S(2)}, u32[]{:S(2)}) collective-permute-start(bf16[2,256,512]{2,1,0:T(8,128)(2,1)} %get-tuple-element.155), channel_id=1, source_target_pairs={{0,3},{1,2},{2,5},{3,4},{4,7},{5,6},{6,9},{7,8},{8,11},{9,10},{10,... | collective-permute-start | bytes 1572872 | tf_op jit(solution)/shard_map/kv_hop_1_0/ppermute | solution.py:344
  10.3 28.7 %collective-permute-start.1 = (bf16[2,256,512]{2,1,0:T(8,128)(2,1)S(1)}, bf16[2,256,512]{2,1,0:T(8,128)(2,1)S(1)}, u32[]{:S(2)}, u32[]{:S(2)}) collective-permute-start(bf16[2,256,512]{2,1,0:T(8,128)(2,1)S(1)} %copy-done.25), channel_id=1, source_target_pairs={{0,2},{1,3},{2,4},{3,5},{4,6},{5,7},{6,8},{7,9},{8,10},{9,11},{10,... | collective-permute-start | bytes 1572872 | tf_op jit(solution)/shard_map/kv_hop_1_0/ppermute | solution.py:344
  35.6 28.4 %collective-permute-start.6 = (bf16[2,2,256,512]{3,2,1,0:T(8,128)(2,1)}, bf16[2,2,256,512]{3,2,1,0:T(8,128)(2,1)S(1)}, u32[]{:S(2)}, u32[]{:S(2)}) collective-permute-start(bf16[2,2,256,512]{3,2,1,0:T(8,128)(2,1)} %get-tuple-element.153.refs_3_.refs_4_), channel_id=1, source_target_pairs={{0,2},{1,3},{2,4},{3,5},{4,6},{5,7},{6,8},{7,9},{8,10},{9,11},{10,... | collective-permute-start | bytes 3145736 | tf_op jit(solution)/shard_map/kv_hop_1_1/ppermute | solution.py:344
  54.1 43.9 %collective-permute-start.5 = (bf16[2,256,1024]{2,1,0:T(8,128)(2,1)}, bf16[2,256,1024]{2,1,0:T(8,128)(2,1)}, u32[]{:S(2)}, u32[]{:S(2)}) collective-permute-start(bf16[2,256,1024]{2,1,0:T(8,128)(2,1)} %get-tuple-element.152), channel_id=1, source_target_pairs={{0,1},{1,0},{2,3},{3,2},{4,5},{5,4},{6,7},{7,6},{8,9},{9,8},{10,11... | collective-permute-start | bytes 3145736 | tf_op jit(solution)/shard_map/qg_swap_0/ppermute | solution.py:338
  55.8 50.2 %collective-permute-start.4 = (bf16[2,2,256,512]{3,2,1,0:T(8,128)(2,1)S(1)}, bf16[2,2,256,512]{3,2,1,0:T(8,128)(2,1)}, u32[]{:S(2)}, u32[]{:S(2)}) collective-permute-start(bf16[2,2,256,512]{3,2,1,0:T(8,128)(2,1)S(1)} %copy-done.21), channel_id=1, source_target_pairs={{0,2},{1,3},{2,4},{3,5},{4,6},{5,7},{6,8},{7,9},{8,10},{9,11},{10,... | collective-permute-start | bytes 3145736 | tf_op jit(solution)/shard_map/kv_hop_1_2/ppermute | solution.py:344
  59.2 49.5 %collective-permute-start.9 = (bf16[2,2,256,512]{3,2,1,0:T(8,128)(2,1)}, bf16[2,2,256,512]{3,2,1,0:T(8,128)(2,1)}, u32[]{:S(2)}, u32[]{:S(2)}) collective-permute-start(bf16[2,2,256,512]{3,2,1,0:T(8,128)(2,1)} %get-tuple-element.167.refs_5_.refs_6_), channel_id=1, source_target_pairs={{0,2},{1,3},{2,4},{3,5},{4,6},{5,7},{6,8},{7,9},{8,10},{9,11},{10,... | collective-permute-start | bytes 3145736 | tf_op jit(solution)/shard_map/kv_hop_2_0/ppermute | solution.py:344
  94.5 38.9 %collective-permute-start.11 = (bf16[2,2,256,512]{3,2,1,0:T(8,128)(2,1)}, bf16[2,2,256,512]{3,2,1,0:T(8,128)(2,1)S(1)}, u32[]{:S(2)}, u32[]{:S(2)}) collective-permute-start(bf16[2,2,256,512]{3,2,1,0:T(8,128)(2,1)} %get-tuple-element.170.refs_3_.refs_4_), channel_id=1, source_target_pairs={{0,2},{1,3},{2,4},{3,5},{4,6},{5,7},{6,8},{7,9},{8,10},{9,11},{10,... | collective-permute-start | bytes 3145736 | tf_op jit(solution)/shard_map/kv_hop_1_3/ppermute | solution.py:344
  100.3 33.1 %collective-permute-start.10 = (bf16[2,256,1024]{2,1,0:T(8,128)(2,1)}, bf16[2,256,1024]{2,1,0:T(8,128)(2,1)}, u32[]{:S(2)}, u32[]{:S(2)}) collective-permute-start(bf16[2,256,1024]{2,1,0:T(8,128)(2,1)} %get-tuple-element.169), channel_id=1, source_target_pairs={{0,1},{1,0},{2,3},{3,2},{4,5},{5,4},{6,7},{7,6},{8,9},{9,8},{10,11... | collective-permute-start | bytes 3145736 | tf_op jit(solution)/shard_map/qg_swap_1/ppermute | solution.py:338
  102.5 51.2 %collective-permute-start.13 = (bf16[2,2,256,512]{3,2,1,0:T(8,128)(2,1)S(1)}, bf16[2,2,256,512]{3,2,1,0:T(8,128)(2,1)}, u32[]{:S(2)}, u32[]{:S(2)}) collective-permute-start(bf16[2,2,256,512]{3,2,1,0:T(8,128)(2,1)S(1)} %collective-permute-done.6.refs_5_.refs_6_), channel_id=1, source_target_pairs={{0,2},{1,3},{2,4},{3,5},{4,6},{5,7},{6,8},{7,9},{8,10},{9,11},{10,... | collective-permute-start | bytes 3145736 | tf_op jit(solution)/shard_map/kv_hop_2_1/ppermute | solution.py:344
  136.0 42.3 %collective-permute-start.12 = (bf16[2,256,1024]{2,1,0:T(8,128)(2,1)}, bf16[2,256,1024]{2,1,0:T(8,128)(2,1)}, u32[]{:S(2)}, u32[]{:S(2)}) collective-permute-start(bf16[2,256,1024]{2,1,0:T(8,128)(2,1)} %get-tuple-element.174), channel_id=1, source_target_pairs={{0,1},{1,0},{2,3},{3,2},{4,5},{5,4},{6,7},{7,6},{8,9},{9,8},{10,11... | collective-permute-start | bytes 3145736 | tf_op jit(solution)/shard_map/qg_swap_2/ppermute | solution.py:338
  137.7 48.9 %collective-permute-start.16 = (bf16[2,2,256,512]{3,2,1,0:T(8,128)(2,1)}, bf16[2,2,256,512]{3,2,1,0:T(8,128)(2,1)}, u32[]{:S(2)}, u32[]{:S(2)}) collective-permute-start(bf16[2,2,256,512]{3,2,1,0:T(8,128)(2,1)} %collective-permute-done.4.refs_5_.refs_6_), channel_id=1, source_target_pairs={{0,2},{1,3},{2,4},{3,5},{4,6},{5,7},{6,8},{7,9},{8,10},{9,11},{10,... | collective-permute-start | bytes 3145736 | tf_op jit(solution)/shard_map/kv_hop_2_2/ppermute | solution.py:344
  141.2 69.9 %collective-permute-start.15 = (bf16[2,2,256,512]{3,2,1,0:T(8,128)(2,1)S(1)}, bf16[2,2,256,512]{3,2,1,0:T(8,128)(2,1)S(1)}, u32[]{:S(2)}, u32[]{:S(2)}) collective-permute-start(bf16[2,2,256,512]{3,2,1,0:T(8,128)(2,1)S(1)} %collective-permute-done.11.refs_5_.refs_6_), channel_id=1, source_target_pairs={{0,2},{1,3},{2,4},{3,5},{4,6},{5,7},{6,8},{7,9},{8,10},{9,11},{10,... | collective-permute-start | bytes 3145736 | tf_op jit(solution)/shard_map/kv_hop_2_3/ppermute | solution.py:344
  180.6 33.4 %collective-permute-start.14 = (bf16[2,256,1024]{2,1,0:T(8,128)(2,1)}, bf16[2,256,1024]{2,1,0:T(8,128)(2,1)}, u32[]{:S(2)}, u32[]{:S(2)}) collective-permute-start(bf16[2,256,1024]{2,1,0:T(8,128)(2,1)} %get-tuple-element.182), channel_id=1, source_target_pairs={{0,1},{1,0},{2,3},{3,2},{4,5},{5,4},{6,7},{7,6},{8,9},{9,8},{10,11... | collective-permute-start | bytes 3145736 | tf_op jit(solution)/shard_map/qg_swap_3/ppermute | solution.py:338
  182.2 31.8 %collective-permute-start.17 = (bf16[2,2,256,512]{3,2,1,0:T(8,128)(2,1)}, bf16[2,2,256,512]{3,2,1,0:T(8,128)(2,1)S(1)}, u32[]{:S(2)}, u32[]{:S(2)}) collective-permute-start(bf16[2,2,256,512]{3,2,1,0:T(8,128)(2,1)} %get-tuple-element.193), channel_id=1, source_target_pairs={{2,0},{3,1},{4,2},{5,3},{6,4},{7,5},{8,6},{9,7},{10,8},{11,9},{12,... | collective-permute-start | bytes 3145736 | tf_op jit(solution)/shard_map/back_1_0/ppermute | solution.py:344
  212.1 47.6 %collective-permute-start.19 = (bf16[2,2,256,512]{3,2,1,0:T(8,128)(2,1)}, bf16[2,2,256,512]{3,2,1,0:T(8,128)(2,1)S(1)}, u32[]{:S(2)}, u32[]{:S(2)}) collective-permute-start(bf16[2,2,256,512]{3,2,1,0:T(8,128)(2,1)} %get-tuple-element.211), channel_id=1, source_target_pairs={{2,0},{3,1},{4,2},{5,3},{6,4},{7,5},{8,6},{9,7},{10,8},{11,9},{12,... | collective-permute-start | bytes 3145736 | tf_op jit(solution)/shard_map/back_1_1/ppermute | solution.py:344
  217.4 38.8 %collective-permute-start.18 = (bf16[1,256,1024]{2,1,0:T(8,128)(2,1)}, bf16[1,256,1024]{2,1,0:T(8,128)(2,1)S(1)}, u32[]{:S(2)}, u32[]{:S(2)}) collective-permute-start(bf16[1,256,1024]{2,1,0:T(8,128)(2,1)} %get-tuple-element.207), channel_id=1, source_target_pairs={{0,1},{1,0},{2,3},{3,2},{4,5},{5,4},{6,7},{7,6},{8,9},{9,8},{10,11... | collective-permute-start | bytes 1572872 | tf_op jit(solution)/shard_map/grad_q_swap_0/ppermute | solution.py:338
  217.8 49.3 %collective-permute-start.20 = (bf16[2,2,256,512]{3,2,1,0:T(8,128)(2,1)}, bf16[2,2,256,512]{3,2,1,0:T(8,128)(2,1)S(1)}, u32[]{:S(2)}, u32[]{:S(2)}) collective-permute-start(bf16[2,2,256,512]{3,2,1,0:T(8,128)(2,1)} %get-tuple-element.215), channel_id=1, source_target_pairs={{2,0},{3,1},{4,2},{5,3},{6,4},{7,5},{8,6},{9,7},{10,8},{11,9},{12,... | collective-permute-start | bytes 3145736 | tf_op jit(solution)/shard_map/back_2_0/ppermute | solution.py:344
  249.8 39.1 %collective-permute-start.22 = (bf16[2,2,256,512]{3,2,1,0:T(8,128)(2,1)}, bf16[2,2,256,512]{3,2,1,0:T(8,128)(2,1)S(1)}, u32[]{:S(2)}, u32[]{:S(2)}) collective-permute-start(bf16[2,2,256,512]{3,2,1,0:T(8,128)(2,1)} %get-tuple-element.223), channel_id=1, source_target_pairs={{2,0},{3,1},{4,2},{5,3},{6,4},{7,5},{8,6},{9,7},{10,8},{11,9},{12,... | collective-permute-start | bytes 3145736 | tf_op jit(solution)/shard_map/back_1_2/ppermute | solution.py:344
  263.1 48.2 %collective-permute-start.25 = (bf16[2,2,256,512]{3,2,1,0:T(8,128)(2,1)}, bf16[2,2,256,512]{3,2,1,0:T(8,128)(2,1)S(1)}, u32[]{:S(2)}, u32[]{:S(2)}) collective-permute-start(bf16[2,2,256,512]{3,2,1,0:T(8,128)(2,1)} %get-tuple-element.235), channel_id=1, source_target_pairs={{2,0},{3,1},{4,2},{5,3},{6,4},{7,5},{8,6},{9,7},{10,8},{11,9},{12,... | collective-permute-start | bytes 3145736 | tf_op jit(solution)/shard_map/back_2_1/ppermute | solution.py:344
  275.6 58.2 %collective-permute-start.28 = (bf16[2,2,256,512]{3,2,1,0:T(8,128)(2,1)}, bf16[2,2,256,512]{3,2,1,0:T(8,128)(2,1)S(1)}, u32[]{:S(2)}, u32[]{:S(2)}) collective-permute-start(bf16[2,2,256,512]{3,2,1,0:T(8,128)(2,1)} %get-tuple-element.245), channel_id=1, source_target_pairs={{2,0},{3,1},{4,2},{5,3},{6,4},{7,5},{8,6},{9,7},{10,8},{11,9},{12,... | collective-permute-start | bytes 3145736 | tf_op jit(solution)/shard_map/back_1_3/ppermute | solution.py:344
  292.4 63.9 %collective-permute-start.30 = (bf16[2,2,256,512]{3,2,1,0:T(8,128)(2,1)}, bf16[2,2,256,512]{3,2,1,0:T(8,128)(2,1)S(1)}, u32[]{:S(2)}, u32[]{:S(2)}) collective-permute-start(bf16[2,2,256,512]{3,2,1,0:T(8,128)(2,1)} %get-tuple-element.253), channel_id=1, source_target_pairs={{2,0},{3,1},{4,2},{5,3},{6,4},{7,5},{8,6},{9,7},{10,8},{11,9},{12,... | collective-permute-start | bytes 3145736 | tf_op jit(solution)/shard_map/back_2_2/ppermute | solution.py:344
  314.7 28.8 %collective-permute-start.29 = (bf16[2,256,512]{2,1,0:T(8,128)(2,1)}, bf16[2,256,512]{2,1,0:T(8,128)(2,1)S(1)}, u32[]{:S(2)}, u32[]{:S(2)}) collective-permute-start(bf16[2,256,512]{2,1,0:T(8,128)(2,1)} %get-tuple-element.248), channel_id=1, source_target_pairs={{0,1},{1,0},{2,3},{3,2},{4,5},{5,4},{6,7},{7,6},{8,9},{9,8},{10,11... | collective-permute-start | bytes 1572872 | tf_op jit(solution)/shard_map/grad_kv_swap_1/ppermute | solution.py:338
  337.2 30.3 %collective-permute-start.31 = (bf16[2,256,512]{2,1,0:T(8,128)(2,1)}, bf16[2,256,512]{2,1,0:T(8,128)(2,1)S(1)}, u32[]{:S(2)}, u32[]{:S(2)}) collective-permute-start(bf16[2,256,512]{2,1,0:T(8,128)(2,1)} %get-tuple-element.255), channel_id=1, source_target_pairs={{2,0},{3,1},{4,2},{5,3},{6,4},{7,5},{8,6},{9,7},{10,8},{11,9},{12,... | collective-permute-start | bytes 1572872 | tf_op jit(solution)/shard_map/back_2_3/ppermute | solution.py:344
  339.1 39.5 %collective-permute-start.32 = (bf16[2,256,512]{2,1,0:T(8,128)(2,1)}, bf16[2,256,512]{2,1,0:T(8,128)(2,1)S(1)}, u32[]{:S(2)}, u32[]{:S(2)}) collective-permute-start(bf16[2,256,512]{2,1,0:T(8,128)(2,1)} %get-tuple-element.257), channel_id=1, source_target_pairs={{2,1},{3,0},{4,3},{5,2},{6,5},{7,4},{8,7},{9,6},{10,9},{11,8},{12,... | collective-permute-start | bytes 1572872 | tf_op jit(solution)/shard_map/back_2_3/ppermute | solution.py:344
  (37 other events, 368.6 us)

commit v3 on v2

--- a/solution.py
+++ b/solution.py
@@ -21,6 +21,7 @@
 exp2_scale = score_scale * math.log2(math.e)
 
 VMEM_LIMIT = 60 * 1024 * 1024
+LAST_GRANT = 63 * 1024 * 1024 + 512 * 1024
 LITTLE = pl.CostEstimate(flops=0, bytes_accessed=1024, transcendentals=0)
 ATTENTION = pl.CostEstimate(flops=10000000000, bytes_accessed=1024, transcendentals=0)
 
@@ -174,7 +175,9 @@
     )(starts, part, token, *operands)
 
 
-def call_copies(kernel, token, part, operands, in_specs, out_specs, out_shape, grid=(1,), aliases=None):
+def call_copies(
+    kernel, token, part, operands, in_specs, out_specs, out_shape, grid=(1,), aliases=None, grant=None
+):
     ins, outs = len(operands), len(out_shape)
 
     def body(part_ref, _, *refs):
@@ -191,7 +194,7 @@
         ),
         out_shape=[jax.ShapeDtypeStruct(token.shape, token.dtype)] + out_shape,
         input_output_aliases={1: 0, **{i + 1: o + 1 for i, o in (aliases or {}).items()}},
-        compiler_params=pltpu.CompilerParams(vmem_limit_bytes=VMEM_LIMIT),
+        compiler_params=pltpu.CompilerParams(vmem_limit_bytes=grant or VMEM_LIMIT),
         cost_estimate=LITTLE,
         name="copies",
     )(part, token, *operands)
@@ -298,7 +301,7 @@
     return token, results[0]
 
 
-def place(token, part, ours, theirs, outs, shape, seq, group, groups):
+def place(token, part, ours, theirs, outs, shape, seq, group, groups, grant=None):
     count, rows, cols = ours[0].shape
     terms = len(ours)
     old = [] if outs is None else list(outs)
@@ -330,6 +333,7 @@
         [jax.ShapeDtypeStruct(shape, jnp.bfloat16)] * count,
         grid=(2,),
         aliases={2 * terms + 1 + n: n for n in range(len(old))},
+        grant=grant,
     )
 
 
@@ -544,7 +548,8 @@
             ours, theirs = [d0[c][0], d0_more[c][0]], [d0_came[c], d0_more[c][1]]
         else:
             ours, theirs = total[c][:1], [total_came[c]]
-        token, outs_kv = place(token, part, ours, theirs, outs_kv, key.shape, *chunks[c])
+        grant = LAST_GRANT if c >= count - 2 else None
+        token, outs_kv = place(token, part, ours, theirs, outs_kv, key.shape, *chunks[c], grant)
 
     stages = [pack_kv, swap_kv, swap_qg, hop_1, hop_2, attend, return_1, return_2]
     stages += [swap_grad_kv, swap_grad_q, put_q, put_kv]

time: 392 us -> 391 us (level)
  the two profiles are of different devices: /device:TPU:10 before, /device:TPU:0 now
where the time goes in v3:
time: 391 us; the launch traced here: 390 us
  Pallas kernels  159 us (41%)
  waiting for transfers between devices  125 us (32%)
  starting transfers between devices  85.6 us (22%)
  local copies, waits for them, and re-layouts  19.4 us (5%)
    pallas_call x4, Pallas kernels, attention(): pl.pallas_call(functools.partial(attention_kernel, pieces), grid_spec=plt...  98.2 us
    ppermute x18, waiting for transfers between devices, shifted(): return lax.ppermute(value, ('ctx', 'fsdp'), pairs)  85.9 us
    ppermute x18, starting transfers between devices, shifted(): return lax.ppermute(value, ('ctx', 'fsdp'), pairs)  64 us
    pallas_call x27, Pallas kernels, call_copies(): pl.pallas_call(body, grid_spec=pltpu.PrefetchScalarGridSpec(num_scalar_pr...  61.2 us
    ppermute x16, waiting for transfers between devices, swapped(): return lax.ppermute(value, 'fsdp', pairs)  38.7 us
    ppermute x16, starting transfers between devices, swapped(): return lax.ppermute(value, 'fsdp', pairs)  21.6 us
    unnamed x48, local copies, waits for them, and re-layouts  16 us
  transfers between devices with their start and end apart: 34, of which 14 were waited for; matrix products, arithmetic and copies ran while one was open for 1% of the time, Pallas kernels for 39%

profile of v3, /device:TPU:0, one launch (start us, length us, event | category | flops | bytes accessed | tf_op | source)
XLA Modules:
  0.0 390.0 jit_solution(13937088515857526849)
XLA Ops:
  8.3 3.4 collective-permute-start.2
  11.8 3.5 collective-permute-start.1
  19.0 7.1 %collective-permute-done.refs_2_ = bf16[2,256,512]{2,1,0:T(8,128)(2,1)S(1)} collective-permute-done((bf16[2,256,512]{2,1,0:T(8,128)(2,1)}, bf16[2,256,512]{2,1,0:T(8,128)(2,1)S(1)}, u32[]{:S(2)}, u32[]{:S(2)}) %collective-permute-start) | collective-permute-done | bytes 524320 | tf_op jit(solution)/shard_map/kv_swap_1/ppermute | solution.py:342
  31.1 9.4 %collective-permute-start.6 = (bf16[2,2,256,512]{3,2,1,0:T(8,128)(2,1)}, bf16[2,2,256,512]{3,2,1,0:T(8,128)(2,1)S(1)}, u32[]{:S(2)}, u32[]{:S(2)}) collective-permute-start(bf16[2,2,256,512]{3,2,1,0:T(8,128)(2,1)} %get-tuple-element.153.refs_3_.refs_4_), channel_id=1, source_target_pairs={{0,2},{1,3},{2,4},{3,5},{4,6},{5,7},{6,8},{7,9},{8,10},{9,11},{10,... | collective-permute-start | bytes 3145736 | tf_op jit(solution)/shard_map/kv_hop_1_1/ppermute | solution.py:348
  51.6 10.1 %collective-permute-start.4 = (bf16[2,2,256,512]{3,2,1,0:T(8,128)(2,1)S(1)}, bf16[2,2,256,512]{3,2,1,0:T(8,128)(2,1)}, u32[]{:S(2)}, u32[]{:S(2)}) collective-permute-start(bf16[2,2,256,512]{3,2,1,0:T(8,128)(2,1)S(1)} %copy-done.18), channel_id=1, source_target_pairs={{0,2},{1,3},{2,4},{3,5},{4,6},{5,7},{6,8},{7,9},{8,10},{9,11},{10,... | collective-permute-start | bytes 3145736 | tf_op jit(solution)/shard_map/kv_hop_1_2/ppermute | solution.py:348
  61.6 3.6 collective-permute-start.9
  66.5 20.2 %collective-permute-done.8.refs_2_ = bf16[2,256,512]{2,1,0:T(8,128)(2,1)S(1)} collective-permute-done((bf16[2,256,512]{2,1,0:T(8,128)(2,1)}, bf16[2,256,512]{2,1,0:T(8,128)(2,1)S(1)}, u32[]{:S(2)}, u32[]{:S(2)}) %collective-permute-start.8) | collective-permute-done | bytes 524320 | tf_op jit(solution)/shard_map/kv_swap_3/ppermute | solution.py:342
  89.7 9.7 %collective-permute-start.11 = (bf16[2,2,256,512]{3,2,1,0:T(8,128)(2,1)}, bf16[2,2,256,512]{3,2,1,0:T(8,128)(2,1)S(1)}, u32[]{:S(2)}, u32[]{:S(2)}) collective-permute-start(bf16[2,2,256,512]{3,2,1,0:T(8,128)(2,1)} %get-tuple-element.170.refs_3_.refs_4_), channel_id=1, source_target_pairs={{0,2},{1,3},{2,4},{3,5},{4,6},{5,7},{6,8},{7,9},{8,10},{9,11},{10,... | collective-permute-start | bytes 3145736 | tf_op jit(solution)/shard_map/kv_hop_1_3/ppermute | solution.py:348
  104.0 4.4 %collective-permute-start.13 = (bf16[2,2,256,512]{3,2,1,0:T(8,128)(2,1)S(1)}, bf16[2,2,256,512]{3,2,1,0:T(8,128)(2,1)}, u32[]{:S(2)}, u32[]{:S(2)}) collective-permute-start(bf16[2,2,256,512]{3,2,1,0:T(8,128)(2,1)S(1)} %collective-permute-done.6.refs_5_.refs_6_), channel_id=1, source_target_pairs={{0,2},{1,3},{2,4},{3,5},{4,6},{5,7},{6,8},{7,9},{8,10},{9,11},{10,... | collective-permute-start | bytes 3145736 | tf_op jit(solution)/shard_map/kv_hop_2_1/ppermute | solution.py:348
  109.3 24.6 %attention.4 = (f32[8,128]{1,0:T(8,128)}, bf16[1,256,1024]{2,1,0:T(8,128)(2,1)}, bf16[1,256,1024]{2,1,0:T(8,128)(2,1)}, bf16[2,2,256,512]{3,2,1,0:T(8,128)(2,1)}...) custom-call(s32[4]{0:T(128)} %get-tuple-element.269.starts, ...), custom_call_target="tpu_custom_call", output_to_operand_aliasing={{0}: (2, {})} | custom-call | flops 10000000000 | bytes 1024 | tf_op jit(solution)/shard_map/attention/pallas_call | solution.py:150
  138.2 5.4 %collective-permute-start.16 = (bf16[2,2,256,512]{3,2,1,0:T(8,128)(2,1)}, bf16[2,2,256,512]{3,2,1,0:T(8,128)(2,1)}, u32[]{:S(2)}, u32[]{:S(2)}) collective-permute-start(bf16[2,2,256,512]{3,2,1,0:T(8,128)(2,1)} %collective-permute-done.4.refs_5_.refs_6_), channel_id=1, source_target_pairs={{0,2},{1,3},{2,4},{3,5},{4,6},{5,7},{6,8},{7,9},{8,10},{9,11},{10,... | collective-permute-start | bytes 3145736 | tf_op jit(solution)/shard_map/kv_hop_2_2/ppermute | solution.py:348
  146.3 7.8 %collective-permute-done.13.refs_7_.refs_8_ = bf16[2,2,256,512]{3,2,1,0:T(8,128)(2,1)} collective-permute-done((bf16[2,2,256,512]{3,2,1,0:T(8,128)(2,1)S(1)}, bf16[2,2,256,512]{3,2,1,0:T(8,128)(2,1)}, u32[]{:S(2)}, u32[]{:S(2)}) %collective-permute-start.13) | collective-permute-done | bytes 1048608 | tf_op jit(solution)/shard_map/kv_hop_2_1/ppermute | solution.py:348
  154.2 24.6 %attention.5 = (f32[8,128]{1,0:T(8,128)}, bf16[1,256,1024]{2,1,0:T(8,128)(2,1)}, bf16[1,256,1024]{2,1,0:T(8,128)(2,1)}, bf16[2,2,256,512]{3,2,1,0:T(8,128)(2,1)}...) custom-call(s32[4]{0:T(128)} %get-tuple-element.269.starts, ...), custom_call_target="tpu_custom_call", output_to_operand_aliasing={{0}: (2, {})} | custom-call | flops 10000000000 | bytes 1024 | tf_op jit(solution)/shard_map/attention/pallas_call | solution.py:150
  183.9 24.5 %attention.6 = (f32[8,128]{1,0:T(8,128)}, bf16[1,256,1024]{2,1,0:T(8,128)(2,1)}, bf16[1,256,1024]{2,1,0:T(8,128)(2,1)}, bf16[2,2,256,512]{3,2,1,0:T(8,128)(2,1)}...) custom-call(s32[4]{0:T(128)} %get-tuple-element.270.starts, ...), custom_call_target="tpu_custom_call", output_to_operand_aliasing={{0}: (2, {})} | custom-call | flops 10000000000 | bytes 1024 | tf_op jit(solution)/shard_map/attention/pallas_call | solution.py:150
  210.7 13.4 %collective-permute-done.17.refs_1_ = bf16[2,2,256,512]{3,2,1,0:T(8,128)(2,1)S(1)} collective-permute-done((bf16[2,2,256,512]{3,2,1,0:T(8,128)(2,1)}, bf16[2,2,256,512]{3,2,1,0:T(8,128)(2,1)S(1)}, u32[]{:S(2)}, u32[]{:S(2)}) %collective-permute-start.17) | collective-permute-done | bytes 1048608 | tf_op jit(solution)/shard_map/back_1_0/ppermute | solution.py:348
  230.6 24.5 %attention.7 = (f32[8,128]{1,0:T(8,128)}, bf16[1,256,1024]{2,1,0:T(8,128)(2,1)}, bf16[1,256,1024]{2,1,0:T(8,128)(2,1)}, bf16[2,2,256,512]{3,2,1,0:T(8,128)(2,1)}...) custom-call(s32[4]{0:T(128)} %get-tuple-element.270.starts, ...), custom_call_target="tpu_custom_call", output_to_operand_aliasing={{0}: (2, {})} | custom-call | flops 10000000000 | bytes 1024 | tf_op jit(solution)/shard_map/attention/pallas_call | solution.py:150
  264.6 4.4 %collective-permute-done.20.refs_1_ = bf16[2,2,256,512]{3,2,1,0:T(8,128)(2,1)S(1)} collective-permute-done((bf16[2,2,256,512]{3,2,1,0:T(8,128)(2,1)}, bf16[2,2,256,512]{3,2,1,0:T(8,128)(2,1)S(1)}, u32[]{:S(2)}, u32[]{:S(2)}) %collective-permute-start.20) | collective-permute-done | bytes 1048608 | tf_op jit(solution)/shard_map/back_2_0/ppermute | solution.py:348
  278.8 12.7 %collective-permute-done.22.refs_1_ = bf16[2,2,256,512]{3,2,1,0:T(8,128)(2,1)S(1)} collective-permute-done((bf16[2,2,256,512]{3,2,1,0:T(8,128)(2,1)}, bf16[2,2,256,512]{3,2,1,0:T(8,128)(2,1)S(1)}, u32[]{:S(2)}, u32[]{:S(2)}) %collective-permute-start.22) | collective-permute-done | bytes 1048608 | tf_op jit(solution)/shard_map/back_1_2/ppermute | solution.py:348
  305.9 8.1 %collective-permute-done.25.refs_1_ = bf16[2,2,256,512]{3,2,1,0:T(8,128)(2,1)S(1)} collective-permute-done((bf16[2,2,256,512]{3,2,1,0:T(8,128)(2,1)}, bf16[2,2,256,512]{3,2,1,0:T(8,128)(2,1)S(1)}, u32[]{:S(2)}, u32[]{:S(2)}) %collective-permute-start.25) | collective-permute-done | bytes 1048608 | tf_op jit(solution)/shard_map/back_2_1/ppermute | solution.py:348
  321.2 8.9 %collective-permute-done.27.refs_2_ = bf16[2,256,512]{2,1,0:T(8,128)(2,1)S(1)} collective-permute-done((bf16[2,256,512]{2,1,0:T(8,128)(2,1)}, bf16[2,256,512]{2,1,0:T(8,128)(2,1)S(1)}, u32[]{:S(2)}, u32[]{:S(2)}) %collective-permute-start.27) | collective-permute-done | bytes 524320 | tf_op jit(solution)/shard_map/grad_kv_swap_3/ppermute | solution.py:342
  330.1 6.3 %collective-permute-done.28.refs_1_ = bf16[2,2,256,512]{3,2,1,0:T(8,128)(2,1)S(1)} collective-permute-done((bf16[2,2,256,512]{3,2,1,0:T(8,128)(2,1)}, bf16[2,2,256,512]{3,2,1,0:T(8,128)(2,1)S(1)}, u32[]{:S(2)}, u32[]{:S(2)}) %collective-permute-start.28) | collective-permute-done | bytes 1048608 | tf_op jit(solution)/shard_map/back_1_3/ppermute | solution.py:348
  345.4 13.5 %collective-permute-done.30.refs_1_ = bf16[2,2,256,512]{3,2,1,0:T(8,128)(2,1)S(1)} collective-permute-done((bf16[2,2,256,512]{3,2,1,0:T(8,128)(2,1)}, bf16[2,2,256,512]{3,2,1,0:T(8,128)(2,1)S(1)}, u32[]{:S(2)}, u32[]{:S(2)}) %collective-permute-start.30) | collective-permute-done | bytes 1048608 | tf_op jit(solution)/shard_map/back_2_2/ppermute | solution.py:348
  363.9 6.3 %collective-permute-done.31.refs_1_ = bf16[2,256,512]{2,1,0:T(8,128)(2,1)} collective-permute-done((bf16[2,256,512]{2,1,0:T(8,128)(2,1)}, bf16[2,256,512]{2,1,0:T(8,128)(2,1)}, u32[]{:S(2)}, u32[]{:S(2)}) %collective-permute-start.31) | collective-permute-done | bytes 524320 | tf_op jit(solution)/shard_map/back_2_3/ppermute | solution.py:348
  370.3 12.4 %collective-permute-done.32.refs_3_ = bf16[2,256,512]{2,1,0:T(8,128)(2,1)} collective-permute-done((bf16[2,256,512]{2,1,0:T(8,128)(2,1)}, bf16[2,256,512]{2,1,0:T(8,128)(2,1)}, u32[]{:S(2)}, u32[]{:S(2)}) %collective-permute-start.32) | collective-permute-done | bytes 524320 | tf_op jit(solution)/shard_map/back_2_3/ppermute | solution.py:348
  (127 shorter events, 120.2 us)
Async XLA Ops:
  8.3 32.2 %collective-permute-start.2 = (bf16[2,256,512]{2,1,0:T(8,128)(2,1)}, bf16[2,256,512]{2,1,0:T(8,128)(2,1)S(1)}, u32[]{:S(2)}, u32[]{:S(2)}) collective-permute-start(bf16[2,256,512]{2,1,0:T(8,128)(2,1)} %get-tuple-element.155), channel_id=1, source_target_pairs={{0,3},{1,2},{2,5},{3,4},{4,7},{5,6},{6,9},{7,8},{8,11},{9,10},{10,... | collective-permute-start | bytes 1572872 | tf_op jit(solution)/shard_map/kv_hop_1_0/ppermute | solution.py:348
  11.8 28.8 %collective-permute-start.1 = (bf16[2,256,512]{2,1,0:T(8,128)(2,1)S(1)}, bf16[2,256,512]{2,1,0:T(8,128)(2,1)S(1)}, u32[]{:S(2)}, u32[]{:S(2)}) collective-permute-start(bf16[2,256,512]{2,1,0:T(8,128)(2,1)S(1)} %copy-done.22), channel_id=1, source_target_pairs={{0,2},{1,3},{2,4},{3,5},{4,6},{5,7},{6,8},{7,9},{8,10},{9,11},{10,... | collective-permute-start | bytes 1572872 | tf_op jit(solution)/shard_map/kv_hop_1_0/ppermute | solution.py:348
  31.0 34.3 %collective-permute-start.7 = (bf16[2,256,512]{2,1,0:T(8,128)(2,1)}, bf16[2,256,512]{2,1,0:T(8,128)(2,1)S(1)}, u32[]{:S(2)}, u32[]{:S(2)}) collective-permute-start(bf16[2,256,512]{2,1,0:T(8,128)(2,1)} %get-tuple-element.155), channel_id=1, source_target_pairs={{0,1},{1,0},{2,3},{3,2},{4,5},{5,4},{6,7},{7,6},{8,9},{9,8},{10,11... | collective-permute-start | bytes 1572872 | tf_op jit(solution)/shard_map/kv_swap_0/ppermute | solution.py:342
  31.1 35.4 %collective-permute-start.6 = (bf16[2,2,256,512]{3,2,1,0:T(8,128)(2,1)}, bf16[2,2,256,512]{3,2,1,0:T(8,128)(2,1)S(1)}, u32[]{:S(2)}, u32[]{:S(2)}) collective-permute-start(bf16[2,2,256,512]{3,2,1,0:T(8,128)(2,1)} %get-tuple-element.153.refs_3_.refs_4_), channel_id=1, source_target_pairs={{0,2},{1,3},{2,4},{3,5},{4,6},{5,7},{6,8},{7,9},{8,10},{9,11},{10,... | collective-permute-start | bytes 3145736 | tf_op jit(solution)/shard_map/kv_hop_1_1/ppermute | solution.py:348
  49.7 49.8 %collective-permute-start.5 = (bf16[2,256,1024]{2,1,0:T(8,128)(2,1)}, bf16[2,256,1024]{2,1,0:T(8,128)(2,1)}, u32[]{:S(2)}, u32[]{:S(2)}) collective-permute-start(bf16[2,256,1024]{2,1,0:T(8,128)(2,1)} %get-tuple-element.152), channel_id=1, source_target_pairs={{0,1},{1,0},{2,3},{3,2},{4,5},{5,4},{6,7},{7,6},{8,9},{9,8},{10,11... | collective-permute-start | bytes 3145736 | tf_op jit(solution)/shard_map/qg_swap_0/ppermute | solution.py:342
  51.6 56.8 %collective-permute-start.4 = (bf16[2,2,256,512]{3,2,1,0:T(8,128)(2,1)S(1)}, bf16[2,2,256,512]{3,2,1,0:T(8,128)(2,1)}, u32[]{:S(2)}, u32[]{:S(2)}) collective-permute-start(bf16[2,2,256,512]{3,2,1,0:T(8,128)(2,1)S(1)} %copy-done.18), channel_id=1, source_target_pairs={{0,2},{1,3},{2,4},{3,5},{4,6},{5,7},{6,8},{7,9},{8,10},{9,11},{10,... | collective-permute-start | bytes 3145736 | tf_op jit(solution)/shard_map/kv_hop_1_2/ppermute | solution.py:348
  61.6 47.7 %collective-permute-start.9 = (bf16[2,2,256,512]{3,2,1,0:T(8,128)(2,1)}, bf16[2,2,256,512]{3,2,1,0:T(8,128)(2,1)}, u32[]{:S(2)}, u32[]{:S(2)}) collective-permute-start(bf16[2,2,256,512]{3,2,1,0:T(8,128)(2,1)} %get-tuple-element.167.refs_5_.refs_6_), channel_id=1, source_target_pairs={{0,2},{1,3},{2,4},{3,5},{4,6},{5,7},{6,8},{7,9},{8,10},{9,11},{10,... | collective-permute-start | bytes 3145736 | tf_op jit(solution)/shard_map/kv_hop_2_0/ppermute | solution.py:348
  89.7 44.1 %collective-permute-start.11 = (bf16[2,2,256,512]{3,2,1,0:T(8,128)(2,1)}, bf16[2,2,256,512]{3,2,1,0:T(8,128)(2,1)S(1)}, u32[]{:S(2)}, u32[]{:S(2)}) collective-permute-start(bf16[2,2,256,512]{3,2,1,0:T(8,128)(2,1)} %get-tuple-element.170.refs_3_.refs_4_), channel_id=1, source_target_pairs={{0,2},{1,3},{2,4},{3,5},{4,6},{5,7},{6,8},{7,9},{8,10},{9,11},{10,... | collective-permute-start | bytes 3145736 | tf_op jit(solution)/shard_map/kv_hop_1_3/ppermute | solution.py:348
  101.8 32.1 %collective-permute-start.10 = (bf16[2,256,1024]{2,1,0:T(8,128)(2,1)}, bf16[2,256,1024]{2,1,0:T(8,128)(2,1)}, u32[]{:S(2)}, u32[]{:S(2)}) collective-permute-start(bf16[2,256,1024]{2,1,0:T(8,128)(2,1)} %get-tuple-element.169), channel_id=1, source_target_pairs={{0,1},{1,0},{2,3},{3,2},{4,5},{5,4},{6,7},{7,6},{8,9},{9,8},{10,11... | collective-permute-start | bytes 3145736 | tf_op jit(solution)/shard_map/qg_swap_1/ppermute | solution.py:342
  104.0 50.2 %collective-permute-start.13 = (bf16[2,2,256,512]{3,2,1,0:T(8,128)(2,1)S(1)}, bf16[2,2,256,512]{3,2,1,0:T(8,128)(2,1)}, u32[]{:S(2)}, u32[]{:S(2)}) collective-permute-start(bf16[2,2,256,512]{3,2,1,0:T(8,128)(2,1)S(1)} %collective-permute-done.6.refs_5_.refs_6_), channel_id=1, source_target_pairs={{0,2},{1,3},{2,4},{3,5},{4,6},{5,7},{6,8},{7,9},{8,10},{9,11},{10,... | collective-permute-start | bytes 3145736 | tf_op jit(solution)/shard_map/kv_hop_2_1/ppermute | solution.py:348
  136.5 42.2 %collective-permute-start.12 = (bf16[2,256,1024]{2,1,0:T(8,128)(2,1)}, bf16[2,256,1024]{2,1,0:T(8,128)(2,1)}, u32[]{:S(2)}, u32[]{:S(2)}) collective-permute-start(bf16[2,256,1024]{2,1,0:T(8,128)(2,1)} %get-tuple-element.174), channel_id=1, source_target_pairs={{0,1},{1,0},{2,3},{3,2},{4,5},{5,4},{6,7},{7,6},{8,9},{9,8},{10,11... | collective-permute-start | bytes 3145736 | tf_op jit(solution)/shard_map/qg_swap_2/ppermute | solution.py:342
  138.2 45.7 %collective-permute-start.16 = (bf16[2,2,256,512]{3,2,1,0:T(8,128)(2,1)}, bf16[2,2,256,512]{3,2,1,0:T(8,128)(2,1)}, u32[]{:S(2)}, u32[]{:S(2)}) collective-permute-start(bf16[2,2,256,512]{3,2,1,0:T(8,128)(2,1)} %collective-permute-done.4.refs_5_.refs_6_), channel_id=1, source_target_pairs={{0,2},{1,3},{2,4},{3,5},{4,6},{5,7},{6,8},{7,9},{8,10},{9,11},{10,... | collective-permute-start | bytes 3145736 | tf_op jit(solution)/shard_map/kv_hop_2_2/ppermute | solution.py:348
  143.6 64.9 %collective-permute-start.15 = (bf16[2,2,256,512]{3,2,1,0:T(8,128)(2,1)S(1)}, bf16[2,2,256,512]{3,2,1,0:T(8,128)(2,1)S(1)}, u32[]{:S(2)}, u32[]{:S(2)}) collective-permute-start(bf16[2,2,256,512]{3,2,1,0:T(8,128)(2,1)S(1)} %collective-permute-done.11.refs_5_.refs_6_), channel_id=1, source_target_pairs={{0,2},{1,3},{2,4},{3,5},{4,6},{5,7},{6,8},{7,9},{8,10},{9,11},{10,... | collective-permute-start | bytes 3145736 | tf_op jit(solution)/shard_map/kv_hop_2_3/ppermute | solution.py:348
  181.0 29.7 %collective-permute-start.14 = (bf16[2,256,1024]{2,1,0:T(8,128)(2,1)}, bf16[2,256,1024]{2,1,0:T(8,128)(2,1)}, u32[]{:S(2)}, u32[]{:S(2)}) collective-permute-start(bf16[2,256,1024]{2,1,0:T(8,128)(2,1)} %get-tuple-element.182), channel_id=1, source_target_pairs={{0,1},{1,0},{2,3},{3,2},{4,5},{5,4},{6,7},{7,6},{8,9},{9,8},{10,11... | collective-permute-start | bytes 3145736 | tf_op jit(solution)/shard_map/qg_swap_3/ppermute | solution.py:342
  182.6 41.5 %collective-permute-start.17 = (bf16[2,2,256,512]{3,2,1,0:T(8,128)(2,1)}, bf16[2,2,256,512]{3,2,1,0:T(8,128)(2,1)S(1)}, u32[]{:S(2)}, u32[]{:S(2)}) collective-permute-start(bf16[2,2,256,512]{3,2,1,0:T(8,128)(2,1)} %get-tuple-element.193), channel_id=1, source_target_pairs={{2,0},{3,1},{4,2},{5,3},{6,4},{7,5},{8,6},{9,7},{10,8},{11,9},{12,... | collective-permute-start | bytes 3145736 | tf_op jit(solution)/shard_map/back_1_0/ppermute | solution.py:348
  209.4 50.4 %collective-permute-start.19 = (bf16[2,2,256,512]{3,2,1,0:T(8,128)(2,1)}, bf16[2,2,256,512]{3,2,1,0:T(8,128)(2,1)S(1)}, u32[]{:S(2)}, u32[]{:S(2)}) collective-permute-start(bf16[2,2,256,512]{3,2,1,0:T(8,128)(2,1)} %get-tuple-element.211), channel_id=1, source_target_pairs={{2,0},{3,1},{4,2},{5,3},{6,4},{7,5},{8,6},{9,7},{10,8},{11,9},{12,... | collective-permute-start | bytes 3145736 | tf_op jit(solution)/shard_map/back_1_1/ppermute | solution.py:348
  227.5 29.0 %collective-permute-start.18 = (bf16[1,256,1024]{2,1,0:T(8,128)(2,1)}, bf16[1,256,1024]{2,1,0:T(8,128)(2,1)S(1)}, u32[]{:S(2)}, u32[]{:S(2)}) collective-permute-start(bf16[1,256,1024]{2,1,0:T(8,128)(2,1)} %get-tuple-element.207), channel_id=1, source_target_pairs={{0,1},{1,0},{2,3},{3,2},{4,5},{5,4},{6,7},{7,6},{8,9},{9,8},{10,11... | collective-permute-start | bytes 1572872 | tf_op jit(solution)/shard_map/grad_q_swap_0/ppermute | solution.py:342
  229.1 39.9 %collective-permute-start.20 = (bf16[2,2,256,512]{3,2,1,0:T(8,128)(2,1)}, bf16[2,2,256,512]{3,2,1,0:T(8,128)(2,1)S(1)}, u32[]{:S(2)}, u32[]{:S(2)}) collective-permute-start(bf16[2,2,256,512]{3,2,1,0:T(8,128)(2,1)} %get-tuple-element.215), channel_id=1, source_target_pairs={{2,0},{3,1},{4,2},{5,3},{6,4},{7,5},{8,6},{9,7},{10,8},{11,9},{12,... | collective-permute-start | bytes 3145736 | tf_op jit(solution)/shard_map/back_2_0/ppermute | solution.py:348
  255.2 36.3 %collective-permute-start.22 = (bf16[2,2,256,512]{3,2,1,0:T(8,128)(2,1)}, bf16[2,2,256,512]{3,2,1,0:T(8,128)(2,1)S(1)}, u32[]{:S(2)}, u32[]{:S(2)}) collective-permute-start(bf16[2,2,256,512]{3,2,1,0:T(8,128)(2,1)} %get-tuple-element.223), channel_id=1, source_target_pairs={{2,0},{3,1},{4,2},{5,3},{6,4},{7,5},{8,6},{9,7},{10,8},{11,9},{12,... | collective-permute-start | bytes 3145736 | tf_op jit(solution)/shard_map/back_1_2/ppermute | solution.py:348
  263.3 50.7 %collective-permute-start.25 = (bf16[2,2,256,512]{3,2,1,0:T(8,128)(2,1)}, bf16[2,2,256,512]{3,2,1,0:T(8,128)(2,1)S(1)}, u32[]{:S(2)}, u32[]{:S(2)}) collective-permute-start(bf16[2,2,256,512]{3,2,1,0:T(8,128)(2,1)} %get-tuple-element.235), channel_id=1, source_target_pairs={{2,0},{3,1},{4,2},{5,3},{6,4},{7,5},{8,6},{9,7},{10,8},{11,9},{12,... | collective-permute-start | bytes 3145736 | tf_op jit(solution)/shard_map/back_2_1/ppermute | solution.py:348
  277.5 58.9 %collective-permute-start.28 = (bf16[2,2,256,512]{3,2,1,0:T(8,128)(2,1)}, bf16[2,2,256,512]{3,2,1,0:T(8,128)(2,1)S(1)}, u32[]{:S(2)}, u32[]{:S(2)}) collective-permute-start(bf16[2,2,256,512]{3,2,1,0:T(8,128)(2,1)} %get-tuple-element.245), channel_id=1, source_target_pairs={{2,0},{3,1},{4,2},{5,3},{6,4},{7,5},{8,6},{9,7},{10,8},{11,9},{12,... | collective-permute-start | bytes 3145736 | tf_op jit(solution)/shard_map/back_1_3/ppermute | solution.py:348
  295.0 63.9 %collective-permute-start.30 = (bf16[2,2,256,512]{3,2,1,0:T(8,128)(2,1)}, bf16[2,2,256,512]{3,2,1,0:T(8,128)(2,1)S(1)}, u32[]{:S(2)}, u32[]{:S(2)}) collective-permute-start(bf16[2,2,256,512]{3,2,1,0:T(8,128)(2,1)} %get-tuple-element.253), channel_id=1, source_target_pairs={{2,0},{3,1},{4,2},{5,3},{6,4},{7,5},{8,6},{9,7},{10,8},{11,9},{12,... | collective-permute-start | bytes 3145736 | tf_op jit(solution)/shard_map/back_2_2/ppermute | solution.py:348
  339.8 30.4 %collective-permute-start.31 = (bf16[2,256,512]{2,1,0:T(8,128)(2,1)}, bf16[2,256,512]{2,1,0:T(8,128)(2,1)}, u32[]{:S(2)}, u32[]{:S(2)}) collective-permute-start(bf16[2,256,512]{2,1,0:T(8,128)(2,1)} %get-tuple-element.255), channel_id=1, source_target_pairs={{2,0},{3,1},{4,2},{5,3},{6,4},{7,5},{8,6},{9,7},{10,8},{11,9},{12,... | collective-permute-start | bytes 1572872 | tf_op jit(solution)/shard_map/back_2_3/ppermute | solution.py:348
  341.1 41.6 %collective-permute-start.32 = (bf16[2,256,512]{2,1,0:T(8,128)(2,1)}, bf16[2,256,512]{2,1,0:T(8,128)(2,1)}, u32[]{:S(2)}, u32[]{:S(2)}) collective-permute-start(bf16[2,256,512]{2,1,0:T(8,128)(2,1)} %get-tuple-element.257), channel_id=1, source_target_pairs={{2,1},{3,0},{4,3},{5,2},{6,5},{7,4},{8,7},{9,6},{10,9},{11,8},{12,... | collective-permute-start | bytes 1572872 | tf_op jit(solution)/shard_map/back_2_3/ppermute | solution.py:348
  (34 other events, 338.3 us)
